TPU v7x, 32 devices: a whole 2x2x4 slice. The times are simulated.
32 devices in a mesh: fsdp: 8 (over y, x, core), tensor: 4 (over z).
Axes of the slice: x: 2, y: 2, z: 4, core: 2. Of those that a mesh axis runs over, the one named last changes fastest.
Arguments:
- saved_weight: float32 [7168, 8192], P(('fsdp', 'tensor')), may hold values from -6 to 6
- saved_first: float32 [7168, 8192], P(('fsdp', 'tensor')), may hold values from -3 to 3
- saved_second: float32 [7168, 8192], P(('fsdp', 'tensor')), may hold values from 0.1 to 2
- saved_order: int32 [7168], P(('fsdp', 'tensor')), may hold values from 0 to 223, as said below
- mask: int32 [7168, 8192], P('tensor', 'fsdp'), may hold values 0 or 1
- hidden: bfloat16 [2048, 7168], P('fsdp', 'tensor'), may hold values from -6 to 6
- cotangent: bfloat16 [2048, 8192], P('fsdp'), may hold values from -6 to 6
Outputs:
- output: bfloat16 [2048, 8192], P('fsdp', 'tensor')
- hidden_grad: bfloat16 [2048, 7168], P('fsdp', 'tensor')
- new_weight: float32 [7168, 8192], P('tensor', 'fsdp')
- new_first: float32 [7168, 8192], P('tensor', 'fsdp')
- new_second: float32 [7168, 8192], P('tensor', 'fsdp')
Inputs may be any that keep to these rules, and one draw needn't show every extreme that they name: `saved_order`: each aligned block of 224 entries holds every number of 0 to 223 once.
All inputs are finite; a program needn't handle non-finite values. No bound on the sum of `mask` on one device may be relied on, other than what follows from the above.
Results may differ from a plain program's by a relative error of at most 0.005.
Values may be sent and summed in bfloat16 or wider, within the bound.
A program may use at most 192 MiB of HBM per device.

v0:
```python
import jax
import jax.numpy as jnp
from jax import lax
from jax.sharding import PartitionSpec as P

R = 7168
STEP = 1000


beta_first = 0.9
beta_second = 0.999
learn_rate = 0.01
decay_rate = 0.1
epsilon = 1e-08


def body(saved_weight, saved_first, saved_second, saved_order, mask, hidden, cotangent):
    band_rows = saved_order.shape[0]
    full_width = saved_weight.shape[1]
    fsdp_count = lax.axis_size("fsdp")
    col_count = full_width // fsdp_count
    inverse = jnp.argsort(saved_order)

    def arrange(saved):
        return jnp.take(saved, inverse, axis=0).reshape(1, 1, band_rows, fsdp_count, col_count)

    moved = (
        lax.all_to_all(
            lax.all_to_all(arrange(saved_weight), "fsdp", split_axis=3, concat_axis=0, tiled=True),
            "tensor",
            split_axis=0,
            concat_axis=1,
            tiled=True,
        ),
        lax.all_to_all(
            lax.all_to_all(arrange(saved_first), "fsdp", split_axis=3, concat_axis=0, tiled=True),
            "tensor",
            split_axis=0,
            concat_axis=1,
            tiled=True,
        ),
        lax.all_to_all(
            lax.all_to_all(arrange(saved_second), "fsdp", split_axis=3, concat_axis=0, tiled=True),
            "tensor",
            split_axis=0,
            concat_axis=1,
            tiled=True,
        ),
    )
    weight = moved[0].reshape(-1, col_count)
    first = moved[1].reshape(-1, col_count)
    second = moved[2].reshape(-1, col_count)
    keep = mask.astype(jnp.float32)
    masked = (weight * keep).astype(jnp.bfloat16)
    scale_alpha = R ** (-0.5)
    tok_rows = hidden.shape[0]
    slab_rows = hidden.shape[1]
    columns = lax.all_gather(masked, "fsdp", axis=1, tiled=True)
    product = jnp.dot(hidden, columns, preferred_element_type=jnp.float32)
    partial_out = product
    grad_rows = lax.dot_general(
        cotangent, columns, (((1,), (1,)), ((), ())), preferred_element_type=jnp.float32
    )
    partial_out, grad_rows = (partial_out, grad_rows)
    output = lax.psum_scatter(
        scale_alpha * partial_out, "tensor", scatter_dimension=1, tiled=True
    ).astype(jnp.bfloat16)
    hidden_grad = (scale_alpha * grad_rows).astype(jnp.bfloat16)
    cot_owned = lax.all_to_all(cotangent, "fsdp", split_axis=1, concat_axis=0, tiled=True)
    hid_piece = lax.all_gather(hidden, "fsdp", axis=0, tiled=True)
    blocks = hid_piece.shape[0] // tok_rows
    hid_blocks = hid_piece.reshape(blocks, tok_rows, slab_rows)
    cot_blocks = cot_owned.reshape(blocks, tok_rows, col_count)
    partials = jnp.einsum(
        "ntr,ntc->nrc", hid_blocks, cot_blocks, preferred_element_type=jnp.float32
    )
    rounded = (scale_alpha * partials).astype(jnp.bfloat16)
    summed = jnp.sum(rounded.astype(jnp.float32), axis=0)
    grad = keep * summed
    new_first = beta_first * first + (1.0 - beta_first) * grad
    new_second = beta_second * second + (1.0 - beta_second) * grad * grad
    corr_first = 1.0 - beta_first ** (STEP + 1)
    corr_second = 1.0 - beta_second ** (STEP + 1)
    update = new_first / corr_first / (jnp.sqrt(new_second / corr_second) + epsilon)
    new_weight = keep * (weight - learn_rate * (update + decay_rate * weight))
    return (output, hidden_grad, new_weight, new_first, new_second)


def solution(mesh):
    return jax.shard_map(
        body,
        mesh=mesh,
        in_specs=(
            P(("fsdp", "tensor"), None),
            P(("fsdp", "tensor"), None),
            P(("fsdp", "tensor"), None),
            P(("fsdp", "tensor")),
            P("tensor", "fsdp"),
            P("fsdp", "tensor"),
            P("fsdp", None),
        ),
        out_specs=(
            P("fsdp", "tensor"),
            P("fsdp", "tensor"),
            P("tensor", "fsdp"),
            P("tensor", "fsdp"),
            P("tensor", "fsdp"),
        ),
        check_vma=False,
    )
```

profile of v0, /device:TPU:15, one launch (start us, length us, event | category | flops | bytes accessed | tf_op | source)
XLA Modules:
  0.0 1198.4 jit_solution(14287890474453403635)
XLA Ops:
  7.2 6.4 copy.31
  13.5 0.0 copy-start.1
  13.5 6.4 copy.32
  20.0 5.3 all-to-all-start.4
  25.3 0.0 copy-done.1
  25.3 3.2 sort.17
  28.4 12.0 gather_fusion.2
  40.4 12.0 gather_fusion.1
  52.4 12.3 %gather_fusion = f32[224,8192]{1,0:T(8,128)} fusion(f32[224,8192]{1,0:T(8,128)} %param.9, s32[1024]{0:T(1024)S(1)} %pad_clamp_fusion), kind=kCustom, calls=%fused_computation.clone | custom fusion | bytes 14680960 | tf_op jit(solution)/shard_map/jit(_take)/gather | solution.py:25
  64.7 13.7 %broadcast_select_fusion.1 = (f32[224,8192]{1,0:T(8,128)}, f32[224,8192]{1,0:T(8,128)S(1)}, f32[224,8192]{1,0:T(8,128)}) fusion(f32[224,8192]{1,0:T(8,128)} %gather_fusion.1, pred[224]{0:T(512)(128)(4,1)S(1)} %compare_and_fusion, f32[224,8192]{1,0:T(8,128)} %gather_fusion.2, f32[224,8192]{1,0:T(8,128)} %gather_fusion), kind=kLoop, calls=%fused_computation.20 | loop fusion | flops 5505024 | bytes 44040416 | tf_op jit(solution)/shard_map/jit(_take)/select_n | solution.py:25
  78.4 7.2 copy.42
  85.6 7.3 copy.34
  92.9 0.0 all-to-all-done.4
  92.9 5.1 all-to-all-start.5
  98.0 10.3 copy.41
  108.3 7.2 copy.28
  115.5 62.7 %all-to-all-done.5 = f32[1,1,224,8,1024]{4,2,1,0,3:T(8,128)} async-done(((f32[1,1,224,8,1024]{4,2,1,0,3:T(8,128)}), f32[1,1,224,8,1024]{4,2,1,0,3:T(8,128)}, u32[]{:S(2)}, u32[]{:S(2)}) %all-to-all-start.5) | async-done | bytes 7340064 | tf_op jit(solution)/shard_map/all_to_all | solution.py:43
  178.2 7.8 all-to-all-start.2
  186.0 10.3 copy.40
  196.3 7.3 copy.25
  203.6 62.5 %all-to-all-done.2 = f32[1,1,224,8,1024]{4,2,1,0,3:T(8,128)} async-done(((f32[1,1,224,8,1024]{4,2,1,0,3:T(8,128)}), f32[1,1,224,8,1024]{4,2,1,0,3:T(8,128)}, u32[]{:S(2)}, u32[]{:S(2)}) %all-to-all-start.2) | async-done | bytes 7340064 | tf_op jit(solution)/shard_map/all_to_all | solution.py:36
  266.1 88.4 %all_to_all.103 = f32[1,1,224,8,1024]{4,2,1,0,3:T(8,128)} all-to-all(f32[1,1,224,8,1024]{4,2,1,0,3:T(8,128)} %copy.25), channel_id=1, replica_groups=mesh['fsdp'=8,'tensor'=4] {'fsdp'}, dimensions={3} | all-to-all | bytes 14680064 | tf_op jit(solution)/shard_map/all_to_all | solution.py:29
  354.5 165.7 %all_to_all.104 = f32[8,1,224,1,1024]{4,2,3,1,0:T(8,128)} all-to-all(f32[8,1,224,1,1024]{4,2,3,1,0:T(8,128)} %bitcast.22), channel_id=1, replica_groups=mesh['fsdp'=8,'tensor'=4] {'tensor'}, dimensions={0} | all-to-all | bytes 14680064 | tf_op jit(solution)/shard_map/all_to_all | solution.py:42
  520.2 7.3 all-to-all-start.3
  527.5 0.0 all-gather.5.cloned.1.call-start
  527.5 0.7 all-gather.5.cloned.1.call-update
  528.2 155.6 %all-to-all-done.3 = f32[8,1,224,1,1024]{4,2,3,1,0:T(8,128)} async-done(((f32[8,1,224,1,1024]{4,2,3,1,0:T(8,128)}), f32[8,1,224,1,1024]{4,2,3,1,0:T(8,128)}, u32[]{:S(2)}, u32[]{:S(2)}) %all-to-all-start.3) | async-done | bytes 7340064 | tf_op jit(solution)/shard_map/all_to_all | solution.py:35
  683.8 0.0 slice-start
  683.8 9.8 all-to-all-start.1
  693.6 0.0 all-gather.3.cloned.1.call-start
  693.6 0.0 all-gather.5.cloned.1.call-done
  693.6 0.0 slice-start.1
  693.6 15.3 %convert_reduce_fusion = f32[1792,1024]{1,0:T(8,128)} fusion(bf16[8,256,1792]{2,1,0:T(8,128)(2,1)} %bitcast.85, bf16[256,8,1024]{2,0,1:T(8,128)(2,1)} %all-to-all-done.4), kind=kOutput, calls=%fused_computation.3 | convolution fusion | flops 7573078016 | bytes 18874368 | tf_op jit(solution)/shard_map/ntr,ntc->nrc/dot_general | solution.py:74
  708.9 0.0 slice-done
  708.9 0.0 slice-done.1
  708.9 0.9 broadcast_multiply_fusion
  709.8 4.3 copy.36
  714.2 4.8 broadcast_multiply_fusion.1
  719.0 4.3 copy.30
  723.3 126.4 %all-to-all-done.1 = f32[8,1,224,1,1024]{4,2,3,1,0:T(8,128)} async-done(((f32[8,1,224,1,1024]{4,2,3,1,0:T(8,128)}), f32[8,1,224,1,1024]{4,2,3,1,0:T(8,128)}, u32[]{:S(2)}, u32[]{:S(2)}) %all-to-all-start.1) | async-done | bytes 7340064 | tf_op jit(solution)/shard_map/all_to_all | solution.py:28
  849.8 7.4 copy.27
  857.2 0.0 copy-start
  857.2 23.8 %fusion.5 = (f32[1792,1024]{1,0:T(8,128)}, f32[1792,1024]{1,0:T(8,128)}, f32[1792,1024]{1,0:T(8,128)}, bf16[1792,1024]{1,0:T(8,128)(2,1)}) fusion(f32[2,4,1,224,1,1024]{5,3,1,0,4,2:T(8,128)} %copy.27, s32[1792,1024]{1,0:T(8,128)} %param.13, f32[1792,1024]{1,0:T(8,128)} %convert_reduce_fusion, f32[2,4,1,224,1,1024]{5,3,1,0,4,2:T(8,128)} %copy.36, ...), kind=kLoop, calls=%fused_computation.16 | loop fusion | flops 31195136 | bytes 62390272 | tf_op jit(solution)/shard_map/mul | solution.py:85
  881.0 0.0 all-gather.3.cloned.1.call-update
  881.0 0.2 reduce-scatter.2.cloned.1.call-start
  881.2 146.4 %all-gather.3.cloned.1.call-done = bf16[1792,8192]{1,0:T(8,128)(2,1)} async-done(((bf16[1792,1024]{1,0:T(8,128)(2,1)}), bf16[1792,8192]{1,0:T(8,128)(2,1)}) %all-gather.3.cloned.1.call-update) | async-done | bytes 29360144 | tf_op jit(solution)/shard_map/all_gather | solution.py:58
  1027.7 0.0 copy-done
  1027.7 16.0 %fusion = f32[256,8192]{0,1:T(8,128)} fusion(bf16[1792,8192]{1,0:T(8,128)(2,1)} %all-gather.3.cloned.1.call-done, bf16[256,1792]{1,0:T(8,128)(2,1)S(1)} %copy-done), kind=kOutput, calls=%fused_computation.7 | convolution fusion | flops 7518289920 | bytes 38666240 | tf_op jit(solution)/shard_map/dot_general | solution.py:59
  1043.6 0.0 reduce-scatter.2.cloned.1.call-update
  1043.7 15.3 %fusion.8 = bf16[256,1792]{0,1:T(8,128)(2,1)S(1)} fusion(bf16[1792,8192]{1,0:T(8,128)(2,1)} %all-gather.3.cloned.1.call-done, bf16[256,8192]{1,0:T(8,128)(2,1)} %param.15), kind=kOutput, calls=%fused_computation.26 | convolution fusion | flops 7517110272 | bytes 34471936 | tf_op jit(solution)/shard_map/dot_general | solution.py:61
  1059.0 1.4 copy.38
  1060.4 128.1 %reduce-scatter.2.cloned.1.call-done = f32[256,2048]{0,1:T(8,128)} async-done(((f32[256,8192]{0,1:T(8,128)}), f32[256,2048]{0,1:T(8,128)}) %reduce-scatter.2.cloned.1.call-update) | async-done | bytes 2097168 | tf_op jit(solution)/shard_map/reduce_scatter | solution.py:65
  1188.5 1.7 convert_element_type.23
  1190.2 1.4 copy.37
  (5 shorter events, 0.0 us)
Async XLA Ops:
  13.5 11.7 copy-start.1
  20.0 72.9 %all-to-all-start.4 = ((bf16[256,8,1024]{2,0,1:T(8,128)(2,1)}), bf16[256,8,1024]{2,0,1:T(8,128)(2,1)}, u32[]{:S(2)}, u32[]{:S(2)}) async-start(bf16[256,8,1024]{2,0,1:T(8,128)(2,1)} %copy.32), calls=%async_computation.5 | async-start | bytes 8388608 | tf_op jit(solution)/shard_map/all_to_all | solution.py:69
  92.9 85.3 %all-to-all-start.5 = ((f32[1,1,224,8,1024]{4,2,1,0,3:T(8,128)}), f32[1,1,224,8,1024]{4,2,1,0,3:T(8,128)}, u32[]{:S(2)}, u32[]{:S(2)}) async-start(f32[1,1,224,8,1024]{4,2,1,0,3:T(8,128)} %copy.34), calls=%async_computation.6 | async-start | bytes 14680064 | tf_op jit(solution)/shard_map/all_to_all | solution.py:43
  178.2 87.9 %all-to-all-start.2 = ((f32[1,1,224,8,1024]{4,2,1,0,3:T(8,128)}), f32[1,1,224,8,1024]{4,2,1,0,3:T(8,128)}, u32[]{:S(2)}, u32[]{:S(2)}) async-start(f32[1,1,224,8,1024]{4,2,1,0,3:T(8,128)} %copy.28), calls=%async_computation.3 | async-start | bytes 14680064 | tf_op jit(solution)/shard_map/all_to_all | solution.py:36
  520.2 163.6 %all-to-all-start.3 = ((f32[8,1,224,1,1024]{4,2,3,1,0:T(8,128)}), f32[8,1,224,1,1024]{4,2,3,1,0:T(8,128)}, u32[]{:S(2)}, u32[]{:S(2)}) async-start(f32[8,1,224,1,1024]{4,2,3,1,0:T(8,128)} %bitcast.12), calls=%async_computation.4 | async-start | bytes 14680064 | tf_op jit(solution)/shard_map/all_to_all | solution.py:35
  527.5 166.1 %all-gather.5.cloned.1.call-start = ((), (), s32[]{:S(2)}) async-start(), calls=%async_computation.10 | async-start | bytes 8257536 | tf_op jit(solution)/shard_map/all_gather | solution.py:70
  683.8 25.1 %slice-start = ((s8[7340032]{0:T(1024)(128)(4,1)}), s8[3145728]{0:T(1024)(128)(4,1)S(1)}, s32[]{:S(2)}) async-start(s8[7340032]{0:T(1024)(128)(4,1)} %bitcast.74), calls=%async_computation.11 | async-start | bytes 6291456
  683.8 166.0 %all-to-all-start.1 = ((f32[8,1,224,1,1024]{4,2,3,1,0:T(8,128)}), f32[8,1,224,1,1024]{4,2,3,1,0:T(8,128)}, u32[]{:S(2)}, u32[]{:S(2)}) async-start(f32[8,1,224,1,1024]{4,2,3,1,0:T(8,128)} %bitcast.73), calls=%async_computation.1 | async-start | bytes 14680064 | tf_op jit(solution)/shard_map/all_to_all | solution.py:28
  693.6 334.0 %all-gather.3.cloned.1.call-start = ((), (), s32[]{:S(2)}) async-start(), calls=%async_computation.8 | async-start | bytes 33030144 | tf_op jit(solution)/shard_map/all_gather | solution.py:58
  693.6 15.3 %slice-start.1 = ((s8[7340032]{0:T(1024)(128)(4,1)}), s8[4194304]{0:T(1024)(128)(4,1)S(1)}, s32[]{:S(2)}) async-start(s8[7340032]{0:T(1024)(128)(4,1)} %bitcast.74), calls=%async_computation.12 | async-start | bytes 8388608
  857.2 170.5 %copy-start = (bf16[256,1792]{1,0:T(8,128)(2,1)S(1)}, bf16[256,1792]{1,0:T(8,128)(2,1)}, u32[]{:S(2)}) copy-start(bf16[256,1792]{1,0:T(8,128)(2,1)} %param.14) | copy-start | bytes 2752516
  881.0 307.5 %reduce-scatter.2.cloned.1.call-start = ((), (), s32[]{:S(2)}) async-start(), calls=%async_computation.9 | async-start | bytes 10485760 | tf_op jit(solution)/shard_map/reduce_scatter | solution.py:65
Sparse Core Ops, SparseCore 0:
  530.2 51.3 all-gather.4
  881.1 146.4 all-gather.2
  1043.8 144.6 reduce-scatter.1
where the time goes:
time: 1220 us; the launch traced here: 1200 us
  waiting for transfers between devices  682 us (56%)
  blocking collectives  254 us (21%)
  local copies, waits for them, and re-layouts  118 us (10%)
  other arithmetic  48.1 us (4%)
  matrix products  46.6 us (4%)
  starting transfers between devices  35.6 us (3%)
  between operations  14 us (1%)
    all_to_all x1, blocking collectives, body(): lax.all_to_all(lax.all_to_all(arrange(saved_second), 'fsdp', split_axis=3...  166 us
    all_to_all x1, waiting for transfers between devices, body(): lax.all_to_all(lax.all_to_all(arrange(saved_first), 'fsdp', split_axis=3,...  156 us
    all_gather x1, waiting for transfers between devices, body(): columns = lax.all_gather(masked, 'fsdp', axis=1, tiled=True)  146 us
    reduce_scatter x1, waiting for transfers between devices, body(): lax.psum_scatter(scale_alpha * partial_out, 'tensor', scatter_dimension=1...  128 us
    all_to_all x1, waiting for transfers between devices, body(): lax.all_to_all(lax.all_to_all(arrange(saved_weight), 'fsdp', split_axis=3...  126 us
    all_to_all x1, blocking collectives, body(): lax.all_to_all(arrange(saved_weight), 'fsdp', split_axis=3, concat_axis=0...  88.4 us
    all_to_all x1, waiting for transfers between devices, body(): lax.all_to_all(arrange(saved_second), 'fsdp', split_axis=3, concat_axis=0...  62.7 us
    all_to_all x1, waiting for transfers between devices, body(): lax.all_to_all(arrange(saved_first), 'fsdp', split_axis=3, concat_axis=0,...  62.5 us
  transfers between devices with their start and end apart: 8, of which 6 were waited for; matrix products, arithmetic and copies ran while one was open for 12% of the time, Pallas kernels for 0%

commit v1 on v0

v1 whole, which is shorter than its diff:
```python
import functools

import jax
import jax.numpy as jnp
from jax import lax
from jax.experimental import pallas as pl
from jax.experimental.pallas import tpu as pltpu
from jax.sharding import PartitionSpec as P

STEP = 1000


beta_first = 0.9
beta_second = 0.999
learn_rate = 0.01
decay_rate = 0.1
epsilon = 1e-08

MESH = pl.DeviceIdType.MESH
ANY = pl.BlockSpec(memory_space=pl.ANY)


def greet(nf, nt):
    f, t = lax.axis_index("fsdp"), lax.axis_index("tensor")
    barrier = pltpu.get_barrier_semaphore()
    for k in range(1, nf):
        pl.semaphore_signal(barrier, inc=1, device_id=(lax.rem(f + k, nf), t), device_id_type=MESH)
    for j in range(1, nt):
        pl.semaphore_signal(barrier, inc=1, device_id=(f, lax.rem(t + j, nt)), device_id_type=MESH)
    pl.semaphore_wait(barrier, nf - 1 + nt - 1)


class Spread:
    def __init__(self, nf, nt, block_of, stage, send, recv):
        self.nf, self.nt, self.block_of, self.stage, self.send, self.recv = nf, nt, block_of, stage, send, recv
        self.f, self.t = lax.axis_index("fsdp"), lax.axis_index("tensor")
        self.sent = []

    def start(self):
        f, t, nf = self.f, self.t, self.nf
        for k in list(range(2, nf)) + [1]:
            to = lax.rem(f + k, nf)
            copy = pltpu.make_async_remote_copy(
                src_ref=self.block_of(to), dst_ref=self.stage.at[f],
                send_sem=self.send.at[k], recv_sem=self.recv.at[k],
                device_id=(to, t), device_id_type=MESH,
            )
            copy.start()
            self.sent.append(copy)
        pltpu.make_async_copy(self.block_of(f), self.stage.at[f], self.recv.at[0]).start()

    def wait_for(self, owner):
        k = lax.rem(self.f - owner + self.nf, self.nf)
        slot = self.stage.at[owner]
        pltpu.make_async_copy(slot, slot, self.recv.at[k]).wait()

    def finish(self):
        for copy in self.sent:
            copy.wait_send()


class Along:
    def __init__(self, nf, nt, stage, out, send, recv, local):
        self.nf, self.nt, self.stage, self.out = nf, nt, stage, out
        self.send, self.recv, self.local = send, recv, local
        self.f, self.t = lax.axis_index("fsdp"), lax.axis_index("tensor")
        self.g = nf // nt
        self.sent, self.kept = [], []

    def start(self, ready):
        f, t, nt, g = self.f, self.t, self.nt, self.g
        for j in list(range(1, nt)) + [0]:
            to = lax.rem(t + j, nt)
            for i in range(g):
                owner = to * g + i
                if ready is not None:
                    ready(owner)
                if j:
                    copy = pltpu.make_async_remote_copy(
                        src_ref=self.stage.at[owner], dst_ref=self.out.at[i, t],
                        send_sem=self.send.at[j, i], recv_sem=self.recv.at[j, i],
                        device_id=(f, to), device_id_type=MESH,
                    )
                    copy.start()
                    self.sent.append(copy)
                else:
                    copy = pltpu.make_async_copy(
                        self.stage.at[owner], self.out.at[i, t], self.local.at[i]
                    )
                    copy.start()
                    self.kept.append(copy)

    def finish(self):
        t, nt = self.t, self.nt
        for j in range(1, nt):
            for i in range(self.g):
                slot = self.out.at[i, lax.rem(t - j + nt, nt)]
                pltpu.make_async_copy(slot, slot, self.recv.at[j, i]).wait()
        for copy in self.sent:
            copy.wait_send()
        for copy in self.kept:
            copy.wait()


class Share:
    def __init__(self, nf, src, out, send, recv, pass_send, pass_recv, local):
        self.nf, self.src, self.out = nf, src, out
        self.send, self.recv, self.pass_send, self.pass_recv, self.local = send, recv, pass_send, pass_recv, local
        self.f, self.t = lax.axis_index("fsdp"), lax.axis_index("tensor")
        self.half = nf // 2
        self.chip, self.core = self.f // 2, lax.rem(self.f, 2)
        self.sent = []

    def start(self):
        f, t, half = self.f, self.t, self.half
        for k in range(1, half):
            to = lax.rem(self.chip + k, half) * 2 + self.core
            copy = pltpu.make_async_remote_copy(
                src_ref=self.src, dst_ref=self.out.at[f], send_sem=self.send.at[k], recv_sem=self.recv.at[k],
                device_id=(to, t), device_id_type=MESH,
            )
            copy.start()
            self.sent.append(copy)
        mate = self.chip * 2 + 1 - self.core
        copy = pltpu.make_async_remote_copy(
            src_ref=self.src, dst_ref=self.out.at[f], send_sem=self.pass_send.at[0], recv_sem=self.pass_recv.at[0],
            device_id=(mate, t), device_id_type=MESH,
        )
        copy.start()
        self.sent.append(copy)
        self.own = pltpu.make_async_copy(self.src, self.out.at[f], self.local.at[0])
        self.own.start()

    def forward(self):
        t, half = self.t, self.half
        mate = self.chip * 2 + 1 - self.core
        for k in range(1, half):
            slot = self.out.at[lax.rem(self.chip - k + half, half) * 2 + self.core]
            pltpu.make_async_copy(slot, slot, self.recv.at[k]).wait()
            copy = pltpu.make_async_remote_copy(
                src_ref=slot, dst_ref=slot, send_sem=self.pass_send.at[k], recv_sem=self.pass_recv.at[k],
                device_id=(mate, t), device_id_type=MESH,
            )
            copy.start()
            self.sent.append(copy)

    def finish(self):
        half = self.half
        for k in range(half):
            slot = self.out.at[lax.rem(self.chip - k + half, half) * 2 + 1 - self.core]
            pltpu.make_async_copy(slot, slot, self.pass_recv.at[k]).wait()
        for copy in self.sent:
            copy.wait_send()
        self.own.wait()


def columns_of(ref, width):
    return lambda to: ref.at[:, pl.ds(pl.multiple_of(to * width, width), width)]


def first_kernel(nf, nt, width, w, m, v, hid, cot, w_stage, m_stage, v_stage, w_out, m_out, hid_out, cot_out,
                 send, recv, z_send, z_recv, local, sh_send, sh_recv, ps_send, ps_recv, sh_local):
    greet(nf, nt)
    spread_w = Spread(nf, nt, columns_of(w, width), w_stage, send.at[0], recv.at[0])
    spread_m = Spread(nf, nt, columns_of(m, width), m_stage, send.at[1], recv.at[1])
    spread_v = Spread(nf, nt, columns_of(v, width), v_stage, send.at[2], recv.at[2])
    spread_c = Spread(nf, nt, columns_of(cot, width), cot_out, send.at[3], recv.at[3])
    along_w = Along(nf, nt, w_stage, w_out, z_send.at[0], z_recv.at[0], local.at[0])
    along_m = Along(nf, nt, m_stage, m_out, z_send.at[1], z_recv.at[1], local.at[1])
    share = Share(nf, hid, hid_out, sh_send, sh_recv, ps_send, ps_recv, sh_local)
    spread_w.start()
    spread_m.start()
    along_w.start(spread_w.wait_for)
    share.start()
    spread_c.start()
    along_m.start(spread_m.wait_for)
    spread_v.start()
    share.forward()
    for owner in range(nf):
        spread_c.wait_for(owner)
    for owner in range(nf):
        spread_v.wait_for(owner)
    share.finish()
    along_w.finish()
    along_m.finish()
    for spread in (spread_w, spread_m, spread_v, spread_c):
        spread.finish()


def second_kernel(nf, nt, v_stage, op, hg, op_stage, v_out, op_out, hg_out, send, recv, z_send, z_recv, local):
    greet(nf, nt)
    spread_o = Spread(nf, nt, lambda to: op.at[to], op_stage, send.at[0], recv.at[0])
    spread_h = Spread(nf, nt, lambda to: hg.at[to], hg_out, send.at[1], recv.at[1])
    along_v = Along(nf, nt, v_stage, v_out, z_send.at[0], z_recv.at[0], local.at[0])
    along_o = Along(nf, nt, op_stage, op_out, z_send.at[1], z_recv.at[1], local.at[1])
    spread_o.start()
    along_v.start(None)
    along_o.start(spread_o.wait_for)
    spread_h.start()
    for owner in range(nf):
        spread_h.wait_for(owner)
    along_v.finish()
    along_o.finish()
    spread_o.finish()
    spread_h.finish()


def body(saved_weight, saved_first, saved_second, saved_order, mask, hidden, cotangent):
    nf, nt = lax.axis_size("fsdp"), lax.axis_size("tensor")
    g = nf // nt
    band = saved_order.shape[0]
    width = saved_weight.shape[1] // nf
    tokens, rows = hidden.shape
    scale = (rows * nt) ** (-0.5)
    f32, bf16 = jnp.float32, jnp.bfloat16

    place = (saved_order[None, :] == jnp.arange(band, dtype=saved_order.dtype)[:, None]).astype(bf16)

    def arrange(saved):
        return jnp.dot(place, saved.astype(bf16), preferred_element_type=f32).astype(bf16)

    w, m, v = arrange(saved_weight), arrange(saved_first), arrange(saved_second)

    def shape(*dims):
        return jax.ShapeDtypeStruct(dims, bf16)

    dma = pltpu.SemaphoreType.DMA
    stage, landed = shape(nf, band, width), shape(g, nt, band, width)
    moved = pl.pallas_call(
        functools.partial(first_kernel, nf, nt, width),
        out_shape=(stage, stage, stage, landed, landed, shape(nf, tokens, rows), shape(nf, tokens, width)),
        in_specs=[ANY] * 5,
        out_specs=(ANY,) * 7,
        scratch_shapes=[
            dma((4, nf)), dma((4, nf)), dma((2, nt, g)), dma((2, nt, g)), dma((2, g)),
            dma((nf // 2,)), dma((nf // 2,)), dma((nf // 2,)), dma((nf // 2,)), dma((1,)),
        ],
        compiler_params=pltpu.CompilerParams(collective_id=0, has_side_effects=True),
        name="relay_weight",
    )(w, m, v, hidden, cotangent)
    v_stage, w_out, m_out, hid_all, cot_all = moved[2:]

    weight = w_out.reshape(rows, width)
    masked = jnp.where(mask != 0, weight, jnp.zeros_like(weight))
    part_out = (scale * jnp.dot(hid_all.reshape(nf * tokens, rows), masked, preferred_element_type=f32)).astype(bf16)
    part_grad = (
        scale
        * lax.dot_general(
            cot_all.reshape(nf * tokens, width), masked, (((1,), (1,)), ((), ())), preferred_element_type=f32
        )
    ).astype(bf16)

    moved = pl.pallas_call(
        functools.partial(second_kernel, nf, nt),
        out_shape=(shape(nf, tokens, width), landed, shape(g, nt, tokens, width), shape(nf, tokens, rows)),
        in_specs=[ANY] * 3,
        out_specs=(ANY,) * 4,
        scratch_shapes=[
            dma((2, nf)), dma((2, nf)), dma((2, nt, g)), dma((2, nt, g)), dma((2, g)),
        ],
        compiler_params=pltpu.CompilerParams(collective_id=1, has_side_effects=True),
        name="relay_products",
    )(v_stage, part_out.reshape(nf, tokens, width), part_grad.reshape(nf, tokens, rows))
    v_out, out_parts, grad_parts = moved[1:]

    output = jnp.sum(out_parts.astype(f32), axis=1).astype(bf16)
    output = output.transpose(1, 0, 2).reshape(tokens, g * width)
    hidden_grad = jnp.sum(grad_parts.astype(f32), axis=0).astype(bf16)

    partials = jnp.einsum("ntr,ntc->nrc", hid_all, cot_all, preferred_element_type=f32)
    summed = jnp.sum((scale * partials).astype(bf16).astype(f32), axis=0)
    keep = mask.astype(f32)
    grad = keep * summed
    first = m_out.reshape(rows, width).astype(f32)
    second = v_out.reshape(rows, width).astype(f32)
    new_first = beta_first * first + (1.0 - beta_first) * grad
    new_second = beta_second * second + (1.0 - beta_second) * grad * grad
    corr_first = 1.0 - beta_first ** (STEP + 1)
    corr_second = 1.0 - beta_second ** (STEP + 1)
    update = new_first / corr_first / (jnp.sqrt(new_second / corr_second) + epsilon)
    new_weight = keep * (weight.astype(f32) - learn_rate * (update + decay_rate * weight.astype(f32)))
    return (output, hidden_grad, new_weight, new_first, new_second)


def solution(mesh):
    return jax.shard_map(
        body,
        mesh=mesh,
        in_specs=(
            P(("fsdp", "tensor"), None),
            P(("fsdp", "tensor"), None),
            P(("fsdp", "tensor"), None),
            P(("fsdp", "tensor")),
            P("tensor", "fsdp"),
            P("fsdp", "tensor"),
            P("fsdp", None),
        ),
        out_specs=(
            P("fsdp", "tensor"),
            P("fsdp", "tensor"),
            P("tensor", "fsdp"),
            P("tensor", "fsdp"),
            P("tensor", "fsdp"),
        ),
        check_vma=False,
    )
```

time: 1220 us -> 475 us (0.39); the launches traced: 1200 us -> 474 us
  waiting for transfers between devices: 682 us -> 0 us
  Pallas kernels: 0 us -> 381 us
  blocking collectives: 254 us -> 0 us
  local copies, waits for them, and re-layouts: 118 us -> 3.07 us
  starting transfers between devices: 35.6 us -> 0 us
  between operations: 14 us -> 0.71 us
    all_to_all x5 -> x0, waiting for transfers between devices: 407 us -> none  [the longest x1 156 us: body(): lax.all_to_all(lax.all_to_all(arrange(saved_first), 'fsdp', split_axis=3,...]
    pallas_call x0 -> x2, Pallas kernels: none -> 381 us  [the longest x1 208 us: body(): pl.pallas_call(functools.partial(first_kernel, nf, nt, width), out_shape=...]
    all_to_all x2 -> x0, blocking collectives: 254 us -> none  [the longest x1 166 us: body(): lax.all_to_all(lax.all_to_all(arrange(saved_second), 'fsdp', split_axis=3...]
    all_gather x2 -> x0, waiting for transfers between devices: 146 us -> none  [the longest x1 146 us: body(): columns = lax.all_gather(masked, 'fsdp', axis=1, tiled=True)]
    reduce_scatter x1 -> x0, waiting for transfers between devices: 128 us -> none  [body(): lax.psum_scatter(scale_alpha * partial_out, 'tensor', scatter_dimension=1...]
    gather x3 -> x0, local copies, waits for them, and re-layouts: 36.2 us -> none  [arrange(): jnp.take(saved, inverse, axis=0)]
    all_to_all x5 -> x0, starting transfers between devices: 35.3 us -> none  [the longest x1 9.83 us: body(): lax.all_to_all(lax.all_to_all(arrange(saved_weight), 'fsdp', split_axis=3...]
    unnamed x14 -> x17, local copies, waits for them, and re-layouts: 37 us -> 2.55 us
  transfers between devices with their start and end apart: 8 -> 0, of which waited for: 6 -> 0; matrix products, arithmetic and copies ran while one was open for 12% -> 0% of each run, Pallas kernels for 0% -> 0%
where the time goes in v1:
time: 475 us; the launch traced here: 474 us
  Pallas kernels  381 us (80%)
  matrix products  46.8 us (10%)
  other arithmetic  42.2 us (9%)
    pallas_call x1, Pallas kernels, body(): pl.pallas_call(functools.partial(first_kernel, nf, nt, width), out_shape=...  208 us
    pallas_call x1, Pallas kernels, body(): pl.pallas_call(functools.partial(second_kernel, nf, nt), out_shape=(shape...  173 us
    mul x1, other arithmetic, body(): keep * (weight.astype(f32) - learn_rate * (update + decay_rate * weight.a...  21.2 us
    dot_general x1, matrix products, body(): jnp.einsum('ntr,ntc->nrc', hid_all, cot_all, preferred_element_type=f32)  15.5 us
    dot_general x3, matrix products, arrange(): jnp.dot(place, saved.astype(bf16), preferred_element_type=f32).astype(bf16)  12.3 us
    dot_general x1, matrix products, body(): lax.dot_general(cot_all.reshape(nf * tokens, width), masked, (((1,), (1,)...  9.78 us

profile of v1, /device:TPU:15, one launch (start us, length us, event | category | flops | bytes accessed | tf_op | source)
XLA Modules:
  0.0 473.6 jit_solution(8828677558351404599)
XLA Ops:
  0.6 0.0 copy-start.3
  0.6 0.0 copy-start
  0.7 0.0 slice-start
  0.7 6.2 %convolution_convert_fusion.2.w = bf16[224,8192]{1,0:T(8,128)(2,1)} fusion(f32[224,8192]{1,0:T(8,128)} %param.7, s32[224]{0:T(256)} %param.10), kind=kOutput, calls=%fused_computation.6 | convolution fusion | flops 825803776 | bytes 11010944 | tf_op jit(solution)/shard_map/dot_general | solution.py:220
  6.9 0.0 copy-done.3
  6.9 0.0 copy-done
  6.9 0.0 slice-start.1
  6.9 3.0 convolution_convert_fusion.1.m
  9.9 0.0 slice-done
  9.9 0.0 slice-done.1
  9.9 3.0 convolution_convert_fusion.v
  12.9 207.8 %relay_weight.1 = (bf16[8,224,1024]{2,1,0:T(8,128)(2,1)}, bf16[8,224,1024]{2,1,0:T(8,128)(2,1)}, bf16[8,224,1024]{2,1,0:T(8,128)(2,1)}, bf16[2,4,224,1024]{3,2,1...) custom-call(bf16[224,8192]{1,0:T(8,128)(2,1)} %convolution_convert_f, ...), custom_call_target="tpu_custom_call" | custom-call | tf_op jit(solution)/shard_map/relay_weight/pallas_call | solution.py:229
  220.8 0.0 copy-start.4
  220.8 5.1 %compare_select_fusion = bf16[1792,1024]{1,0:T(8,128)(2,1)S(1)} fusion(s32[1792,1024]{1,0:T(8,128)} %param.11, bf16[2,4,224,1024]{3,2,1,0:T(8,128)(2,1)} %get-tuple-element.15), kind=kLoop, calls=%fused_computation.18 | loop fusion | flops 3670016 | bytes 14680064 | tf_op jit(solution)/shard_map/jit(_where)/select_n | solution.py:244
  225.9 1.1 copy-done.4
  227.0 0.0 copy-start.5
  227.0 9.2 %multiply_convert_fusion.2 = bf16[2048,1024]{1,0:T(8,128)(2,1)} fusion(bf16[2048,1792]{1,0:T(8,128)(2,1)S(1)} %bitcast.27, bf16[1792,1024]{1,0:T(8,128)(2,1)S(1)} %compare_select_fusion), kind=kOutput, calls=%fused_computation.9 | convolution fusion | flops 7520387072 | bytes 15204352 | tf_op jit(solution)/shard_map/dot_general | solution.py:245
  236.2 0.0 copy-done.5
  236.2 9.8 %multiply_convert_fusion.1 = bf16[2048,1792]{1,0:T(8,128)(2,1)} fusion(bf16[2048,1024]{1,0:T(8,128)(2,1)S(1)} %bitcast.28, bf16[1792,1024]{1,0:T(8,128)(2,1)S(1)} %compare_select_fusion), kind=kOutput, calls=%fused_computation.2 | convolution fusion | flops 7523532800 | bytes 15204352 | tf_op jit(solution)/shard_map/dot_general | solution.py:248
  246.0 173.0 %relay_products.1 = (bf16[8,256,1024]{2,1,0:T(8,128)(2,1)}, bf16[2,4,224,1024]{3,2,1,0:T(8,128)(2,1)}, bf16[2,4,256,1024]{3,2,1,0:T(8,128)(2,1)}, bf16[8,256,1792]{2,1,0:T(8,128)(2,1)}) custom-call(bf16[8,224,1024]{2,1,0:T(8,128)(2,1)} %get-tuple-element.13.v_stage, bf16[8,256,1024]{2,1,0:T(8,128)(2,1)} %bitcast.26, bf16[8,256,1792]{2,1,0:T(8,128)(2,1)} %bitcast.23), custom_call_target="tpu_custom_call" | custom-call | tf_op jit(solution)/shard_map/relay_products/pallas_call | solution.py:253
  419.0 3.3 reduce_sum.33
  422.3 5.3 %reduce_sum.34 = bf16[256,1792]{1,0:T(8,128)(2,1)} reduce(bf16[8,256,1792]{2,1,0:T(8,128)(2,1)} %get-tuple-element.18, bf16[]{:T(256)} %constant.12.clone.1), dimensions={0}, to_apply=%region_1.2 | reduce | flops 3211264 | bytes 8257538 | tf_op jit(solution)/shard_map/reduce_sum | solution.py:268
  427.6 0.5 copy.14
  428.1 1.4 copy.16
  429.5 0.0 copy-start.1
  429.5 0.0 copy-start.2
  429.5 15.5 %convert_reduce_fusion = f32[1792,1024]{1,0:T(8,128)} fusion(bf16[8,256,1792]{2,1,0:T(8,128)(2,1)} %get-tuple-element.14, bf16[8,256,1024]{2,1,0:T(8,128)(2,1)} %get-tuple-element.16), kind=kOutput, calls=%fused_computation | convolution fusion | flops 7573078016 | bytes 18874368 | tf_op jit(solution)/shard_map/ntr,ntc->nrc/dot_general | solution.py:270
  445.1 0.0 copy-done.1
  445.1 0.0 copy-done.2
  445.1 7.3 %convert_multiply_fusion.1 = (f32[2,4,224,1024]{3,2,1,0:T(8,128)}, f32[2,4,224,1024]{3,2,1,0:T(8,128)}) fusion(bf16[2,4,224,1024]{3,2,1,0:T(8,128)(2,1)S(1)} %copy-done.2, bf16[2,4,224,1024]{3,2,1,0:T(8,128)(2,1)S(1)} %copy-done.1), kind=kLoop, calls=%fused_computation.15 | loop fusion | flops 7340032 | bytes 22020096 | tf_op jit(solution)/shard_map/mul | solution.py:277
  452.4 21.2 %fusion.2 = (f32[1792,1024]{1,0:T(8,128)}, f32[1792,1024]{1,0:T(8,128)}, f32[1792,1024]{1,0:T(8,128)}) fusion(s32[1792,1024]{1,0:T(8,128)} %param.11, bf16[2,4,224,1024]{3,2,1,0:T(8,128)(2,1)} %get-tuple-element.15, f32[1792,1024]{1,0:T(8,128)} %convert_reduce_fusion, f32[2,4,224,1024]{3,2,1,0:T(8,128)} %get-tuple-element.29, ...), kind=kLoop, calls=%fused_computation.12 | loop fusion | flops 29360128 | bytes 55050240 | tf_op jit(solution)/shard_map/mul | solution.py:281
  (1 shorter events, 0.0 us)
Async XLA Ops:
  0.6 6.3 %copy-start.3 = (s32[224]{0:T(256)S(1)}, s32[224]{0:T(256)}, u32[]{:S(2)}) copy-start(s32[224]{0:T(256)} %param.10) | copy-start | bytes 2692
  0.6 6.3 %copy-start = (f32[224,8192]{1,0:T(8,128)S(1)}, f32[224,8192]{1,0:T(8,128)}, u32[]{:S(2)}) copy-start(f32[224,8192]{1,0:T(8,128)} %param.8) | copy-start | bytes 22020100
  0.7 9.3 %slice-start = ((s8[7340032]{0:T(1024)(128)(4,1)}), s8[4194304]{0:T(1024)(128)(4,1)S(1)}, s32[]{:S(2)}) async-start(s8[7340032]{0:T(1024)(128)(4,1)} %bitcast.21), calls=%async_computation | async-start | bytes 8388608
  6.9 3.0 slice-start.1
  220.8 6.2 %copy-start.4 = (bf16[8,256,1792]{2,1,0:T(8,128)(2,1)S(1)}, bf16[8,256,1792]{2,1,0:T(8,128)(2,1)}, u32[]{:S(2)}) copy-start(bf16[8,256,1792]{2,1,0:T(8,128)(2,1)} %get-tuple-element.14) | copy-start | bytes 22020100
  227.0 9.2 %copy-start.5 = (bf16[8,256,1024]{2,1,0:T(8,128)(2,1)S(1)}, bf16[8,256,1024]{2,1,0:T(8,128)(2,1)}, u32[]{:S(2)}) copy-start(bf16[8,256,1024]{2,1,0:T(8,128)(2,1)} %get-tuple-element.16) | copy-start | bytes 12582916
  429.5 15.5 %copy-start.1 = (bf16[2,4,224,1024]{3,2,1,0:T(8,128)(2,1)S(1)}, bf16[2,4,224,1024]{3,2,1,0:T(8,128)(2,1)}, u32[]{:S(2)}) copy-start(bf16[2,4,224,1024]{3,2,1,0:T(8,128)(2,1)} %get-tuple-element.19) | copy-start | bytes 11010052
  429.5 15.5 %copy-start.2 = (bf16[2,4,224,1024]{3,2,1,0:T(8,128)(2,1)S(1)}, bf16[2,4,224,1024]{3,2,1,0:T(8,128)(2,1)}, u32[]{:S(2)}) copy-start(bf16[2,4,224,1024]{3,2,1,0:T(8,128)(2,1)} %get-tuple-element.20) | copy-start | bytes 11010052

commit v2 on v1

--- a/solution.py
+++ b/solution.py
@@ -31,28 +31,27 @@
 
 
 class Spread:
-    def __init__(self, nf, nt, block_of, stage, send, recv):
-        self.nf, self.nt, self.block_of, self.stage, self.send, self.recv = nf, nt, block_of, stage, send, recv
-        self.f, self.t = lax.axis_index("fsdp"), lax.axis_index("tensor")
+    def __init__(self, count, me, device_of, block_of, stage, send, recv):
+        self.count, self.me, self.device_of = count, me, device_of
+        self.block_of, self.stage, self.send, self.recv = block_of, stage, send, recv
         self.sent = []
 
     def start(self):
-        f, t, nf = self.f, self.t, self.nf
-        for k in list(range(2, nf)) + [1]:
-            to = lax.rem(f + k, nf)
+        me, count = self.me, self.count
+        for k in list(range(2, count)) + [1]:
+            to = lax.rem(me + k, count)
             copy = pltpu.make_async_remote_copy(
-                src_ref=self.block_of(to), dst_ref=self.stage.at[f],
+                src_ref=self.block_of(to), dst_ref=self.stage.at[me],
                 send_sem=self.send.at[k], recv_sem=self.recv.at[k],
-                device_id=(to, t), device_id_type=MESH,
+                device_id=self.device_of(to), device_id_type=MESH,
             )
             copy.start()
             self.sent.append(copy)
-        pltpu.make_async_copy(self.block_of(f), self.stage.at[f], self.recv.at[0]).start()
+        pltpu.make_async_copy(self.block_of(me), self.stage.at[me], self.recv.at[0]).start()
 
     def wait_for(self, owner):
-        k = lax.rem(self.f - owner + self.nf, self.nf)
         slot = self.stage.at[owner]
-        pltpu.make_async_copy(slot, slot, self.recv.at[k]).wait()
+        pltpu.make_async_copy(slot, slot, self.recv.at[lax.rem(self.me - owner + self.count, self.count)]).wait()
 
     def finish(self):
         for copy in self.sent:
@@ -90,16 +89,23 @@
                     copy.start()
                     self.kept.append(copy)
 
-    def finish(self):
+    def arrive(self, after=None):
         t, nt = self.t, self.nt
         for j in range(1, nt):
             for i in range(self.g):
-                slot = self.out.at[i, lax.rem(t - j + nt, nt)]
+                owner = lax.rem(t - j + nt, nt)
+                slot = self.out.at[i, owner]
                 pltpu.make_async_copy(slot, slot, self.recv.at[j, i]).wait()
+                if after is not None:
+                    after(i, j, owner)
+        for i in range(self.g):
+            self.kept[i].wait()
+            if after is not None:
+                after(i, 0, t)
+
+    def finish(self):
         for copy in self.sent:
             copy.wait_send()
-        for copy in self.kept:
-            copy.wait()
 
 
 class Share:
@@ -154,55 +160,123 @@
         self.own.wait()
 
 
-def columns_of(ref, width):
-    return lambda to: ref.at[:, pl.ds(pl.multiple_of(to * width, width), width)]
-
-
-def first_kernel(nf, nt, width, w, m, v, hid, cot, w_stage, m_stage, v_stage, w_out, m_out, hid_out, cot_out,
-                 send, recv, z_send, z_recv, local, sh_send, sh_recv, ps_send, ps_recv, sh_local):
+def columns_of(ref, width, start, size):
+    return lambda to: ref.at[:, pl.ds(pl.multiple_of(to * width + start, 128), size)]
+
+
+def first_kernel(nf, nt, width, w, m, v, keep, hid, cot,
+                 w_stage, m_stage, v_stage, w_out, m_out, v_out, hid_out, cot_out, w_mate, cot_mate, keep_mate,
+                 send, recv, z_send, z_recv, local, sh_send, sh_recv, ps_send, ps_recv, sh_local,
+                 mw_send, mw_recv, mc_send, mc_recv, mk_send, mk_recv):
+    f, t = lax.axis_index("fsdp"), lax.axis_index("tensor")
+    core = lax.rem(f, 2)
+    mate = (f + 1 - 2 * core, t)
     greet(nf, nt)
-    spread_w = Spread(nf, nt, columns_of(w, width), w_stage, send.at[0], recv.at[0])
-    spread_m = Spread(nf, nt, columns_of(m, width), m_stage, send.at[1], recv.at[1])
-    spread_v = Spread(nf, nt, columns_of(v, width), v_stage, send.at[2], recv.at[2])
-    spread_c = Spread(nf, nt, columns_of(cot, width), cot_out, send.at[3], recv.at[3])
+
+    def spread(ref, start, size, stage, n):
+        return Spread(
+            nf, f, lambda to: (to, t), columns_of(ref, width, start, size), stage, send.at[n], recv.at[n]
+        )
+
+    def to_mate(src, dst, send_sem, recv_sem):
+        copy = pltpu.make_async_remote_copy(
+            src_ref=src, dst_ref=dst, send_sem=send_sem, recv_sem=recv_sem, device_id=mate, device_id_type=MESH
+        )
+        copy.start()
+        return copy
+
+    spread_w = spread(w, 0, width, w_stage, 0)
+    spread_m = spread(m, 0, width, m_stage, 1)
+    spread_v = spread(v, 0, width // 2, v_stage, 2)
+    spread_c = spread(cot, 0, width, cot_out, 3)
     along_w = Along(nf, nt, w_stage, w_out, z_send.at[0], z_recv.at[0], local.at[0])
     along_m = Along(nf, nt, m_stage, m_out, z_send.at[1], z_recv.at[1], local.at[1])
+    along_v = Along(nf, nt, v_stage, v_out, z_send.at[2], z_recv.at[2], local.at[2])
     share = Share(nf, hid, hid_out, sh_send, sh_recv, ps_send, ps_recv, sh_local)
+    passed = []
     spread_w.start()
     spread_m.start()
+    passed.append(to_mate(keep, keep_mate, mk_send.at[0], mk_recv.at[0]))
     along_w.start(spread_w.wait_for)
     share.start()
     spread_c.start()
     along_m.start(spread_m.wait_for)
     spread_v.start()
     share.forward()
+    along_v.start(spread_v.wait_for)
+
+    def pass_weight(i, j, owner):
+        passed.append(to_mate(w_out.at[i, owner], w_mate.at[i, owner], mw_send.at[j, i], mw_recv.at[j, i]))
+
+    along_w.arrive(pass_weight)
     for owner in range(nf):
         spread_c.wait_for(owner)
-    for owner in range(nf):
-        spread_v.wait_for(owner)
+    for n in range(nf // 2):
+        theirs = 2 * n + 1 - core
+        passed.append(to_mate(cot_out.at[theirs], cot_mate.at[n], mc_send.at[n], mc_recv.at[n]))
     share.finish()
-    along_w.finish()
-    along_m.finish()
-    for spread in (spread_w, spread_m, spread_v, spread_c):
-        spread.finish()
-
-
-def second_kernel(nf, nt, v_stage, op, hg, op_stage, v_out, op_out, hg_out, send, recv, z_send, z_recv, local):
+    for copy in passed:
+        copy.wait()
+    along_m.arrive()
+    along_v.arrive()
+    for part in (spread_w, spread_m, spread_v, spread_c, along_w, along_m, along_v):
+        part.finish()
+
+
+def second_kernel(nf, nt, width, v, op, hg, v_stage, op_stage, v_out, op_out, hg_out,
+                  send, recv, z_send, z_recv, local):
+    f, t = lax.axis_index("fsdp"), lax.axis_index("tensor")
+    chip, core = f // 2, lax.rem(f, 2)
     greet(nf, nt)
-    spread_o = Spread(nf, nt, lambda to: op.at[to], op_stage, send.at[0], recv.at[0])
-    spread_h = Spread(nf, nt, lambda to: hg.at[to], hg_out, send.at[1], recv.at[1])
+    everyone = lambda to: (to, t)
+    spread_v = Spread(
+        nf, f, everyone, columns_of(v, width, width // 2, width // 2), v_stage, send.at[0], recv.at[0]
+    )
+    spread_o = Spread(nf, f, everyone, lambda to: op.at[to], op_stage, send.at[1], recv.at[1])
+    spread_h = Spread(
+        nf // 2, chip, lambda to: (to * 2 + core, t), lambda to: hg.at[to], hg_out, send.at[2], recv.at[2]
+    )
     along_v = Along(nf, nt, v_stage, v_out, z_send.at[0], z_recv.at[0], local.at[0])
     along_o = Along(nf, nt, op_stage, op_out, z_send.at[1], z_recv.at[1], local.at[1])
+    spread_v.start()
     spread_o.start()
-    along_v.start(None)
+    along_v.start(spread_v.wait_for)
     along_o.start(spread_o.wait_for)
     spread_h.start()
-    for owner in range(nf):
+    for owner in range(nf // 2):
         spread_h.wait_for(owner)
-    along_v.finish()
-    along_o.finish()
-    spread_o.finish()
-    spread_h.finish()
+    along_v.arrive()
+    along_o.arrive()
+    for part in (spread_v, spread_o, spread_h, along_v, along_o):
+        part.finish()
+
+
+def step_kernel(scale, hid, cot, mask, w, m, va, vb, new_w, new_m, new_v):
+    f32 = jnp.float32
+    blocks, _, width = cot.shape
+    piece = width // 4
+    corr_first = 1.0 - beta_first ** (STEP + 1)
+    corr_second = 1.0 - beta_second ** (STEP + 1)
+    for c in range(4):
+        cols = slice(c * piece, (c + 1) * piece)
+        total = None
+        for n in range(blocks):
+            part = lax.dot_general(
+                hid[n], cot[n, :, cols], (((0,), (0,)), ((), ())), preferred_element_type=f32
+            )
+            part = (scale * part).astype(jnp.bfloat16).astype(f32)
+            total = part if total is None else total + part
+        kept = mask[:, cols] != 0
+        grad = jnp.where(kept, total, 0.0)
+        half = slice((c % 2) * piece, (c % 2 + 1) * piece)
+        second = (va if c < 2 else vb)[:, half].astype(f32)
+        weight = w[:, cols].astype(f32)
+        first = beta_first * m[:, cols].astype(f32) + (1.0 - beta_first) * grad
+        second = beta_second * second + (1.0 - beta_second) * grad * grad
+        update = (first * (1.0 / corr_first)) / (jnp.sqrt(second * (1.0 / corr_second)) + epsilon)
+        new_m[:, cols] = first
+        new_v[:, cols] = second
+        new_w[:, cols] = jnp.where(kept, weight - learn_rate * (update + decay_rate * weight), 0.0)
 
 
 def body(saved_weight, saved_first, saved_second, saved_order, mask, hidden, cotangent):
@@ -225,60 +299,81 @@
         return jax.ShapeDtypeStruct(dims, bf16)
 
     dma = pltpu.SemaphoreType.DMA
+    half = width // 2
     stage, landed = shape(nf, band, width), shape(g, nt, band, width)
+    stage_half, landed_half = shape(nf, band, half), shape(g, nt, band, half)
+    keep = mask.astype(bf16)
     moved = pl.pallas_call(
         functools.partial(first_kernel, nf, nt, width),
-        out_shape=(stage, stage, stage, landed, landed, shape(nf, tokens, rows), shape(nf, tokens, width)),
-        in_specs=[ANY] * 5,
-        out_specs=(ANY,) * 7,
+        out_shape=(
+            stage, stage, stage_half, landed, landed, landed_half, shape(nf, tokens, rows), shape(nf, tokens, width),
+            landed, shape(nf // 2, tokens, width), shape(rows, width),
+        ),
+        in_specs=[ANY] * 6,
+        out_specs=(ANY,) * 11,
         scratch_shapes=[
-            dma((4, nf)), dma((4, nf)), dma((2, nt, g)), dma((2, nt, g)), dma((2, g)),
+            dma((4, nf)), dma((4, nf)), dma((3, nt, g)), dma((3, nt, g)), dma((3, g)),
             dma((nf // 2,)), dma((nf // 2,)), dma((nf // 2,)), dma((nf // 2,)), dma((1,)),
+            dma((nt, g)), dma((nt, g)), dma((nf // 2,)), dma((nf // 2,)), dma((1,)), dma((1,)),
         ],
         compiler_params=pltpu.CompilerParams(collective_id=0, has_side_effects=True),
         name="relay_weight",
-    )(w, m, v, hidden, cotangent)
-    v_stage, w_out, m_out, hid_all, cot_all = moved[2:]
+    )(w, m, v, keep, hidden, cotangent)
+    w_out, m_out, va_out, hid_all, cot_all, w_mate, cot_mate, keep_mate = moved[3:]
 
     weight = w_out.reshape(rows, width)
-    masked = jnp.where(mask != 0, weight, jnp.zeros_like(weight))
+    masked = weight * keep
+    masked_mate = w_mate.reshape(rows, width) * keep_mate
     part_out = (scale * jnp.dot(hid_all.reshape(nf * tokens, rows), masked, preferred_element_type=f32)).astype(bf16)
-    part_grad = (
-        scale
-        * lax.dot_general(
-            cot_all.reshape(nf * tokens, width), masked, (((1,), (1,)), ((), ())), preferred_element_type=f32
+    core = lax.rem(lax.axis_index("fsdp"), 2)
+    cot_own = lax.dynamic_index_in_dim(cot_all.reshape(nf // 2, 2, tokens, width), core, 1, keepdims=False)
+
+    def back(cot, masked):
+        return lax.dot_general(
+            cot.reshape(nf // 2 * tokens, width), masked, (((1,), (1,)), ((), ())), preferred_element_type=f32
         )
-    ).astype(bf16)
+
+    part_grad = (scale * (back(cot_own, masked) + back(cot_mate, masked_mate))).astype(bf16)
 
     moved = pl.pallas_call(
-        functools.partial(second_kernel, nf, nt),
-        out_shape=(shape(nf, tokens, width), landed, shape(g, nt, tokens, width), shape(nf, tokens, rows)),
+        functools.partial(second_kernel, nf, nt, width),
+        out_shape=(
+            stage_half, shape(nf, tokens, width), landed_half, shape(g, nt, tokens, width),
+            shape(nf // 2, tokens, rows),
+        ),
         in_specs=[ANY] * 3,
-        out_specs=(ANY,) * 4,
+        out_specs=(ANY,) * 5,
         scratch_shapes=[
-            dma((2, nf)), dma((2, nf)), dma((2, nt, g)), dma((2, nt, g)), dma((2, g)),
+            dma((3, nf)), dma((3, nf)), dma((2, nt, g)), dma((2, nt, g)), dma((2, g)),
         ],
         compiler_params=pltpu.CompilerParams(collective_id=1, has_side_effects=True),
         name="relay_products",
-    )(v_stage, part_out.reshape(nf, tokens, width), part_grad.reshape(nf, tokens, rows))
-    v_out, out_parts, grad_parts = moved[1:]
+    )(v, part_out.reshape(nf, tokens, width), part_grad.reshape(nf // 2, tokens, rows))
+    vb_out, out_parts, grad_parts = moved[2:]
 
     output = jnp.sum(out_parts.astype(f32), axis=1).astype(bf16)
     output = output.transpose(1, 0, 2).reshape(tokens, g * width)
     hidden_grad = jnp.sum(grad_parts.astype(f32), axis=0).astype(bf16)
 
-    partials = jnp.einsum("ntr,ntc->nrc", hid_all, cot_all, preferred_element_type=f32)
-    summed = jnp.sum((scale * partials).astype(bf16).astype(f32), axis=0)
-    keep = mask.astype(f32)
-    grad = keep * summed
-    first = m_out.reshape(rows, width).astype(f32)
-    second = v_out.reshape(rows, width).astype(f32)
-    new_first = beta_first * first + (1.0 - beta_first) * grad
-    new_second = beta_second * second + (1.0 - beta_second) * grad * grad
-    corr_first = 1.0 - beta_first ** (STEP + 1)
-    corr_second = 1.0 - beta_second ** (STEP + 1)
-    update = new_first / corr_first / (jnp.sqrt(new_second / corr_second) + epsilon)
-    new_weight = keep * (weight.astype(f32) - learn_rate * (update + decay_rate * weight.astype(f32)))
+    tile = 256 if rows % 256 == 0 else 128
+    whole = lambda cols: pl.BlockSpec((tile, cols), lambda r: (r, 0))
+    result = jax.ShapeDtypeStruct((rows, width), f32)
+    new_weight, new_first, new_second = pl.pallas_call(
+        functools.partial(step_kernel, scale),
+        grid=(rows // tile,),
+        out_shape=(result,) * 3,
+        in_specs=[
+            pl.BlockSpec((nf, tokens, tile), lambda r: (0, 0, r)),
+            pl.BlockSpec((nf, tokens, width), lambda r: (0, 0, 0)),
+            whole(width), whole(width), whole(width), whole(half), whole(half),
+        ],
+        out_specs=(whole(width),) * 3,
+        compiler_params=pltpu.CompilerParams(vmem_limit_bytes=48 * 2**20),
+        name="grad_and_step",
+    )(
+        hid_all, cot_all, mask, weight, m_out.reshape(rows, width),
+        va_out.reshape(rows, half), vb_out.reshape(rows, half),
+    )
     return (output, hidden_grad, new_weight, new_first, new_second)
 
 

time: 475 us -> 469 us (0.987)
  other arithmetic: 42.2 us -> 10.7 us
  Pallas kernels: 381 us -> 411 us
  matrix products: 46.8 us -> 37.6 us
  local copies, waits for them, and re-layouts: 3.07 us -> 8.46 us
    pallas_call x1, Pallas kernels: 208 us -> 236 us  [body(): pl.pallas_call(functools.partial(first_kernel, nf, nt, width), out_shape=...]
    mul x2 -> x1, other arithmetic: 28.5 us -> 0.61 us  [body(): masked_mate = w_mate.reshape(rows, width) * keep_mate]
    dot_general x2, matrix products: 25.3 us -> 11.6 us  [back(): lax.dot_general(cot.reshape(nf // 2 * tokens, width), masked, (((1,), (1,...]
    select_n x1 -> x0, other arithmetic: 5.11 us -> none  [body(): masked = jnp.where(mask != 0, weight, jnp.zeros_like(weight))]
    pallas_call x1 -> x2, Pallas kernels: 173 us -> 175 us  [the longest x1 151 us: body(): pl.pallas_call(functools.partial(second_kernel, nf, nt, width), out_shape...]
where the time goes in v2:
time: 469 us; the launch traced here: 468 us
  Pallas kernels  411 us (88%)
  matrix products  37.6 us (8%)
  other arithmetic  10.7 us (2%)
  local copies, waits for them, and re-layouts  8.46 us (2%)
    pallas_call x1, Pallas kernels, body(): pl.pallas_call(functools.partial(first_kernel, nf, nt, width), out_shape=...  236 us
    pallas_call x1, Pallas kernels, body(): pl.pallas_call(functools.partial(second_kernel, nf, nt, width), out_shape...  151 us
    pallas_call x1, Pallas kernels, body(): pl.pallas_call(functools.partial(step_kernel, scale), grid=(rows // tile,...  24.5 us
    dot_general x1, matrix products, body(): jnp.dot(hid_all.reshape(nf * tokens, rows), masked, preferred_element_typ...  13.7 us
    dot_general x3, matrix products, arrange(): jnp.dot(place, saved.astype(bf16), preferred_element_type=f32).astype(bf16)  12.2 us
    dot_general x2, matrix products, back(): lax.dot_general(cot.reshape(nf // 2 * tokens, width), masked, (((1,), (1,...  11.6 us

profile of v2, /device:TPU:15, one launch (start us, length us, event | category | flops | bytes accessed | tf_op | source)
XLA Modules:
  0.0 468.5 jit_solution(17363970860113587786)
XLA Ops:
  0.6 0.0 copy-start.7
  0.6 0.0 copy-start.3
  0.7 6.2 %convolution_convert_fusion.2.v = bf16[224,8192]{1,0:T(8,128)(2,1)} fusion(f32[224,8192]{1,0:T(8,128)} %param.9, s32[224]{0:T(256)} %param.10), kind=kOutput, calls=%fused_computation.2 | convolution fusion | flops 825803776 | bytes 11010944 | tf_op jit(solution)/shard_map/dot_general | solution.py:294
  6.9 0.0 copy-done.7
  6.9 0.0 copy-done.3
  6.9 0.0 copy-start.4
  6.9 0.0 slice-start
  6.9 3.0 convolution_convert_fusion.1.w
  9.9 1.3 copy-done.4
  11.3 0.0 slice-start.1
  11.3 3.0 convolution_convert_fusion.m
  14.3 0.0 slice-done
  14.3 0.0 slice-done.1
  14.3 3.0 convert_element_type.38.keep
  17.2 235.9 %relay_weight.1 = (bf16[8,224,1024]{2,1,0:T(8,128)(2,1)}, bf16[8,224,1024]{2,1,0:T(8,128)(2,1)}, bf16[8,224,512]{2,1,0:T(8,128)(2,1)}, bf16[2,4,224,1024]{3,2,1,...) custom-call(bf16[224,8192]{1,0:T(8,128)(2,1)} %convolution_convert_f, ...), custom_call_target="tpu_custom_call" | custom-call | tf_op jit(solution)/shard_map/relay_weight/pallas_call | solution.py:306
  253.1 13.7 %multiply_convert_fusion = bf16[2048,1024]{1,0:T(8,128)(2,1)} fusion(bf16[2048,1792]{1,0:T(8,128)(2,1)} %bitcast.23, bf16[1792,1024]{1,0:T(8,128)(2,1)} %bitcast.27, bf16[1792,1024]{1,0:T(8,128)(2,1)} %convert_element_type.38.keep), kind=kOutput, calls=%fused_computation.3 | convolution fusion | flops 7522222080 | bytes 18874368 | tf_op jit(solution)/shard_map/dot_general | solution.py:327
  266.8 0.0 copy-start.2
  266.8 1.9 constant_dynamic-slice_fusion
  268.8 0.7 copy-done.2
  269.5 0.0 copy-start.5
  269.5 0.0 copy-start.6
  269.5 6.2 %fusion.3 = f32[1024,1792]{1,0:T(8,128)S(1)} fusion(bf16[1024,1024]{1,0:T(8,128)(2,1)S(1)} %bitcast.32, bf16[1792,1024]{1,0:T(8,128)(2,1)} %bitcast.28, bf16[1792,1024]{1,0:T(8,128)(2,1)S(1)} %copy-done.2), kind=kOutput, calls=%fused_computation.9 | convolution fusion | flops 3759931392 | bytes 16777216 | tf_op jit(solution)/shard_map/dot_general | solution.py:332
  275.7 0.0 copy-done.5
  275.7 0.0 copy-done.6
  275.7 0.0 copy-start.8
  275.7 0.6 bitcast_multiply_fusion
  276.4 1.0 copy-done.8
  277.3 5.5 %multiply_convert_fusion.1 = bf16[1024,1792]{1,0:T(8,128)(2,1)} fusion(f32[1024,1792]{1,0:T(8,128)S(1)} %fusion.3, bf16[1024,1024]{1,0:T(8,128)(2,1)S(1)} %bitcast.33, bf16[1792,1024]{1,0:T(8,128)(2,1)S(1)} %bitcast_multiply_fusion), kind=kOutput, calls=%fused_computation.4 | convolution fusion | flops 3763601408 | bytes 16777216 | tf_op jit(solution)/shard_map/dot_general | solution.py:332
  282.8 150.6 %relay_products.1 = (bf16[8,224,512]{2,1,0:T(8,128)(2,1)}, bf16[8,256,1024]{2,1,0:T(8,128)(2,1)}, bf16[2,4,224,512]{3,2,1,0:T(8,128)(2,1)}, bf16[2,4,256,1024]{3,2,1,0:T(8,128)(2,1)}, bf16[4,256,1792]{2,1,0:T(8,128)(2,1)}) custom-call(bf16[224,8192]{1,0:T(8,128)(2,1)} %convolution_convert_fusion.2.v, bf16[8,256,1024]{2,1,0:T(8,128)(2,1)} %bitcast.26, ...), custom_call_target="tpu_custom_call" | custom-call | tf_op jit(solution)/shard_map/relay_products/pallas_call | solution.py:338
  433.4 3.3 reduce_sum.24
  436.8 0.5 copy.12
  437.3 0.0 copy-start
  437.3 1.4 copy.13
  438.7 3.8 reduce_sum.25
  442.5 0.0 copy-done
  442.5 0.0 copy-start.1
  442.5 1.5 copy-done.1
  444.0 24.5 %grad_and_step.1 = (f32[1792,1024]{1,0:T(8,128)}, f32[1792,1024]{1,0:T(8,128)}, f32[1792,1024]{1,0:T(8,128)}) custom-call(bf16[8,256,1792]{2,1,0:T(8,128)(2,1)} %get-tuple-element.19.hid, bf16[8,256,1024]{2,1,0:T(8,128)(2,1)} %get-tuple-element.21.cot, s32[1792,1024]{1,0:T(8,128)} %mask.1, bf16[1792,1024]{1,0:T(8,128)(2,1)} %bitcast.29, ...), custom_call_target="tpu_custom_call" | custom-call | tf_op jit(solution)/shard_map/grad_and_step/pallas_call | solution.py:361
  (1 shorter events, 0.0 us)
Async XLA Ops:
  0.6 6.2 %copy-start.7 = (s32[224]{0:T(256)S(1)}, s32[224]{0:T(256)}, u32[]{:S(2)}) copy-start(s32[224]{0:T(256)} %param.10) | copy-start | bytes 2692
  0.6 6.2 %copy-start.3 = (f32[224,8192]{1,0:T(8,128)S(1)}, f32[224,8192]{1,0:T(8,128)}, u32[]{:S(2)}) copy-start(f32[224,8192]{1,0:T(8,128)} %param.7) | copy-start | bytes 22020100
  6.9 4.4 copy-start.4
  6.9 7.4 %slice-start = ((s8[7340032]{0:T(1024)(128)(4,1)}), s8[4194304]{0:T(1024)(128)(4,1)S(1)}, s32[]{:S(2)}) async-start(s8[7340032]{0:T(1024)(128)(4,1)} %bitcast.20), calls=%async_computation | async-start | bytes 8388608
  11.3 3.0 slice-start.1
  266.8 2.7 copy-start.2
  269.5 6.2 %copy-start.5 = (bf16[2,4,224,1024]{3,2,1,0:T(8,128)(2,1)S(1)}, bf16[2,4,224,1024]{3,2,1,0:T(8,128)(2,1)}, u32[]{:S(2)}) copy-start(bf16[2,4,224,1024]{3,2,1,0:T(8,128)(2,1)} %get-tuple-element.23) | copy-start | bytes 11010052
  269.5 6.2 %copy-start.6 = (bf16[1792,1024]{1,0:T(8,128)(2,1)S(1)}, bf16[1792,1024]{1,0:T(8,128)(2,1)}, u32[]{:S(2)}) copy-start(bf16[1792,1024]{1,0:T(8,128)(2,1)} %get-tuple-element.24) | copy-start | bytes 11010052
  275.7 1.6 copy-start.8
  437.3 5.2 %copy-start = (bf16[2,4,224,512]{3,2,1,0:T(8,128)(2,1)S(1)}, bf16[2,4,224,512]{3,2,1,0:T(8,128)(2,1)}, u32[]{:S(2)}) copy-start(bf16[2,4,224,512]{3,2,1,0:T(8,128)(2,1)} %get-tuple-element.28) | copy-start | bytes 5505028
  442.5 1.5 copy-start.1

commit v3 on v2

--- a/solution.py
+++ b/solution.py
@@ -165,7 +165,7 @@
 
 
 def first_kernel(nf, nt, width, w, m, v, keep, hid, cot,
-                 w_stage, m_stage, v_stage, w_out, m_out, v_out, hid_out, cot_out, w_mate, cot_mate, keep_mate,
+                 w_stage, m_stage, v_stage, w_out, m_out, v_out, hid_out, cot_out, w_mate, cot_mate, keep_mate, v_later,
                  send, recv, z_send, z_recv, local, sh_send, sh_recv, ps_send, ps_recv, sh_local,
                  mw_send, mw_recv, mc_send, mc_recv, mk_send, mk_recv):
     f, t = lax.axis_index("fsdp"), lax.axis_index("tensor")
@@ -189,6 +189,7 @@
     spread_m = spread(m, 0, width, m_stage, 1)
     spread_v = spread(v, 0, width // 2, v_stage, 2)
     spread_c = spread(cot, 0, width, cot_out, 3)
+    spread_l = spread(v, width // 2, width // 4, v_later, 4)
     along_w = Along(nf, nt, w_stage, w_out, z_send.at[0], z_recv.at[0], local.at[0])
     along_m = Along(nf, nt, m_stage, m_out, z_send.at[1], z_recv.at[1], local.at[1])
     along_v = Along(nf, nt, v_stage, v_out, z_send.at[2], z_recv.at[2], local.at[2])
@@ -204,6 +205,7 @@
     spread_v.start()
     share.forward()
     along_v.start(spread_v.wait_for)
+    spread_l.start()
 
     def pass_weight(i, j, owner):
         passed.append(to_mate(w_out.at[i, owner], w_mate.at[i, owner], mw_send.at[j, i], mw_recv.at[j, i]))
@@ -219,20 +221,24 @@
         copy.wait()
     along_m.arrive()
     along_v.arrive()
-    for part in (spread_w, spread_m, spread_v, spread_c, along_w, along_m, along_v):
+    for owner in range(nf):
+        spread_l.wait_for(owner)
+    for part in (spread_w, spread_m, spread_v, spread_c, spread_l, along_w, along_m, along_v):
         part.finish()
 
 
-def second_kernel(nf, nt, width, v, op, hg, v_stage, op_stage, v_out, op_out, hg_out,
+def second_kernel(nf, nt, width, v, op, hg, v_stage, op_stage, v_out, op_out, hg_out, op_later,
                   send, recv, z_send, z_recv, local):
     f, t = lax.axis_index("fsdp"), lax.axis_index("tensor")
     chip, core = f // 2, lax.rem(f, 2)
     greet(nf, nt)
     everyone = lambda to: (to, t)
     spread_v = Spread(
-        nf, f, everyone, columns_of(v, width, width // 2, width // 2), v_stage, send.at[0], recv.at[0]
+        nf, f, everyone, columns_of(v, width, width // 2 + width // 4, width // 4), v_stage, send.at[0], recv.at[0]
     )
-    spread_o = Spread(nf, f, everyone, lambda to: op.at[to], op_stage, send.at[1], recv.at[1])
+    now, later = op_stage.shape[1], op_later.shape[1]
+    spread_o = Spread(nf, f, everyone, lambda to: op.at[to, pl.ds(0, now)], op_stage, send.at[1], recv.at[1])
+    spread_l = Spread(nf, f, everyone, lambda to: op.at[to, pl.ds(now, later)], op_later, send.at[3], recv.at[3])
     spread_h = Spread(
         nf // 2, chip, lambda to: (to * 2 + core, t), lambda to: hg.at[to], hg_out, send.at[2], recv.at[2]
     )
@@ -242,16 +248,19 @@
     spread_o.start()
     along_v.start(spread_v.wait_for)
     along_o.start(spread_o.wait_for)
+    spread_l.start()
     spread_h.start()
+    for owner in range(nf):
+        spread_l.wait_for(owner)
     for owner in range(nf // 2):
         spread_h.wait_for(owner)
     along_v.arrive()
     along_o.arrive()
-    for part in (spread_v, spread_o, spread_h, along_v, along_o):
+    for part in (spread_v, spread_o, spread_l, spread_h, along_v, along_o):
         part.finish()
 
 
-def step_kernel(scale, hid, cot, mask, w, m, va, vb, new_w, new_m, new_v):
+def step_kernel(scale, hid, cot, mask, w, m, va, vl, vb, new_w, new_m, new_v):
     f32 = jnp.float32
     blocks, _, width = cot.shape
     piece = width // 4
@@ -268,8 +277,7 @@
             total = part if total is None else total + part
         kept = mask[:, cols] != 0
         grad = jnp.where(kept, total, 0.0)
-        half = slice((c % 2) * piece, (c % 2 + 1) * piece)
-        second = (va if c < 2 else vb)[:, half].astype(f32)
+        second = (va[:, cols] if c < 2 else vl[...] if c == 2 else vb[...]).astype(f32)
         weight = w[:, cols].astype(f32)
         first = beta_first * m[:, cols].astype(f32) + (1.0 - beta_first) * grad
         second = beta_second * second + (1.0 - beta_second) * grad * grad
@@ -298,7 +306,21 @@
     def shape(*dims):
         return jax.ShapeDtypeStruct(dims, bf16)
 
+    def hop(stage):
+        slots = stage.reshape((nt, g) + stage.shape[1:])
+        pick = lambda j: lax.dynamic_index_in_dim(slots, lax.rem(t + j, nt), 0, keepdims=False)
+        return [pick(0)] + [
+            lax.ppermute(pick(j), "tensor", [(n, (n + j) % nt) for n in range(nt)]) for j in range(1, nt)
+        ]
+
+    def arranged(pieces):
+        stacked = jnp.stack(pieces)
+        return [
+            lax.dynamic_index_in_dim(stacked, lax.rem(t - n + nt, nt), 0, keepdims=False) for n in range(nt)
+        ]
+
     dma = pltpu.SemaphoreType.DMA
+    t = lax.axis_index("tensor")
     half = width // 2
     stage, landed = shape(nf, band, width), shape(g, nt, band, width)
     stage_half, landed_half = shape(nf, band, half), shape(g, nt, band, half)
@@ -308,18 +330,20 @@
         out_shape=(
             stage, stage, stage_half, landed, landed, landed_half, shape(nf, tokens, rows), shape(nf, tokens, width),
             landed, shape(nf // 2, tokens, width), shape(rows, width),
+            shape(nf, band, width // 4),
         ),
         in_specs=[ANY] * 6,
-        out_specs=(ANY,) * 11,
+        out_specs=(ANY,) * 12,
         scratch_shapes=[
-            dma((4, nf)), dma((4, nf)), dma((3, nt, g)), dma((3, nt, g)), dma((3, g)),
+            dma((5, nf)), dma((5, nf)), dma((3, nt, g)), dma((3, nt, g)), dma((3, g)),
             dma((nf // 2,)), dma((nf // 2,)), dma((nf // 2,)), dma((nf // 2,)), dma((1,)),
             dma((nt, g)), dma((nt, g)), dma((nf // 2,)), dma((nf // 2,)), dma((1,)), dma((1,)),
         ],
         compiler_params=pltpu.CompilerParams(collective_id=0, has_side_effects=True),
         name="relay_weight",
     )(w, m, v, keep, hidden, cotangent)
-    w_out, m_out, va_out, hid_all, cot_all, w_mate, cot_mate, keep_mate = moved[3:]
+    w_out, m_out, va_out, hid_all, cot_all, w_mate, cot_mate, keep_mate, v_later = moved[3:]
+    vl_out = jnp.stack(arranged(hop(v_later)), axis=1)
 
     weight = w_out.reshape(rows, width)
     masked = weight * keep
@@ -335,24 +359,25 @@
 
     part_grad = (scale * (back(cot_own, masked) + back(cot_mate, masked_mate))).astype(bf16)
 
+    later = tokens * 3 // 8 // 16 * 16
+    now = tokens - later
     moved = pl.pallas_call(
         functools.partial(second_kernel, nf, nt, width),
         out_shape=(
-            stage_half, shape(nf, tokens, width), landed_half, shape(g, nt, tokens, width),
-            shape(nf // 2, tokens, rows),
+            shape(nf, band, width // 4), shape(nf, now, width), shape(g, nt, band, width // 4),
+            shape(g, nt, now, width), shape(nf // 2, tokens, rows), shape(nf, later, width),
         ),
         in_specs=[ANY] * 3,
-        out_specs=(ANY,) * 5,
+        out_specs=(ANY,) * 6,
         scratch_shapes=[
-            dma((3, nf)), dma((3, nf)), dma((2, nt, g)), dma((2, nt, g)), dma((2, g)),
+            dma((4, nf)), dma((4, nf)), dma((2, nt, g)), dma((2, nt, g)), dma((2, g)),
         ],
         compiler_params=pltpu.CompilerParams(collective_id=1, has_side_effects=True),
         name="relay_products",
     )(v, part_out.reshape(nf, tokens, width), part_grad.reshape(nf // 2, tokens, rows))
-    vb_out, out_parts, grad_parts = moved[2:]
-
-    output = jnp.sum(out_parts.astype(f32), axis=1).astype(bf16)
-    output = output.transpose(1, 0, 2).reshape(tokens, g * width)
+    vb_out, out_parts, grad_parts, out_later = moved[2:]
+    out_later = hop(out_later)
+
     hidden_grad = jnp.sum(grad_parts.astype(f32), axis=0).astype(bf16)
 
     tile = 256 if rows % 256 == 0 else 128
@@ -365,15 +390,22 @@
         in_specs=[
             pl.BlockSpec((nf, tokens, tile), lambda r: (0, 0, r)),
             pl.BlockSpec((nf, tokens, width), lambda r: (0, 0, 0)),
-            whole(width), whole(width), whole(width), whole(half), whole(half),
+            whole(width), whole(width), whole(width), whole(half), whole(width // 4), whole(width // 4),
         ],
         out_specs=(whole(width),) * 3,
         compiler_params=pltpu.CompilerParams(vmem_limit_bytes=48 * 2**20),
+        cost_estimate=pl.CostEstimate(
+            flops=2 * nf * tokens * rows * width, bytes_accessed=50 * rows * width // 2, transcendentals=rows * width
+        ),
         name="grad_and_step",
     )(
         hid_all, cot_all, mask, weight, m_out.reshape(rows, width),
-        va_out.reshape(rows, half), vb_out.reshape(rows, half),
+        va_out.reshape(rows, half), vl_out.reshape(rows, width // 4), vb_out.reshape(rows, width // 4),
     )
+    output = jnp.concatenate(
+        [jnp.sum(out_parts.astype(f32), axis=1), sum(piece.astype(f32) for piece in out_later)], axis=1
+    ).astype(bf16)
+    output = output.transpose(1, 0, 2).reshape(tokens, g * width)
     return (output, hidden_grad, new_weight, new_first, new_second)
 
 

time: 469 us -> 436 us (0.930)
  Pallas kernels: 411 us -> 364 us
  starting transfers between devices: 0 us -> 4.94 us
    pallas_call x1, Pallas kernels: 151 us -> 103 us  [body(): pl.pallas_call(functools.partial(second_kernel, nf, nt, width), out_shape...]
    ppermute x0 -> x6, starting transfers between devices: none -> 4.94 us  [hop(): lax.ppermute(pick(j), 'tensor', [(n, (n + j) % nt) for n in range(nt)])]
  transfers between devices with their start and end apart: 0 -> 6, of which waited for: 0 -> 0; matrix products, arithmetic and copies ran while one was open for 0% -> 9% of each run, Pallas kernels for 0% -> 30%
where the time goes in v3:
time: 436 us; the launch traced here: 431 us
  Pallas kernels  364 us (83%)
  matrix products  37.3 us (9%)
  other arithmetic  12.7 us (3%)
  local copies, waits for them, and re-layouts  11.7 us (3%)
  starting transfers between devices  4.94 us (1%)
    pallas_call x1, Pallas kernels, body(): pl.pallas_call(functools.partial(first_kernel, nf, nt, width), out_shape=...  236 us
    pallas_call x1, Pallas kernels, body(): pl.pallas_call(functools.partial(second_kernel, nf, nt, width), out_shape...  103 us
    pallas_call x1, Pallas kernels, body(): pl.pallas_call(functools.partial(step_kernel, scale), grid=(rows // tile,...  24.5 us
    dot_general x1, matrix products, body(): jnp.dot(hid_all.reshape(nf * tokens, rows), masked, preferred_element_typ...  13.5 us
    dot_general x3, matrix products, arrange(): jnp.dot(place, saved.astype(bf16), preferred_element_type=f32).astype(bf16)  12.2 us
    dot_general x2, matrix products, back(): lax.dot_general(cot.reshape(nf // 2 * tokens, width), masked, (((1,), (1,...  11.6 us
  transfers between devices with their start and end apart: 6, of which 0 were waited for; matrix products, arithmetic and copies ran while one was open for 9% of the time, Pallas kernels for 30%

profile of v3, /device:TPU:15, one launch (start us, length us, event | category | flops | bytes accessed | tf_op | source)
XLA Modules:
  0.0 431.3 jit_solution(7294246701436513993)
XLA Ops:
  0.7 0.0 copy-start.3
  0.7 0.0 copy-start.7
  0.7 6.2 %convolution_convert_fusion.2.v = bf16[224,8192]{1,0:T(8,128)(2,1)} fusion(f32[224,8192]{1,0:T(8,128)} %param.9, s32[224]{0:T(256)} %param.10), kind=kOutput, calls=%fused_computation.2 | convolution fusion | flops 825803776 | bytes 11010944 | tf_op jit(solution)/shard_map/dot_general | solution.py:302
  6.9 0.0 copy-done.3
  6.9 0.0 copy-done.7
  6.9 0.0 copy-start.4
  6.9 0.0 slice-start
  6.9 3.0 convolution_convert_fusion.1.w
  9.9 1.4 copy-done.4
  11.3 0.0 slice-start.1
  11.3 3.0 convolution_convert_fusion.m
  14.3 0.0 slice-done
  14.3 0.0 slice-done.1
  14.3 3.0 convert_element_type.55.keep
  17.2 236.1 %relay_weight.1 = (bf16[8,224,1024]{2,1,0:T(8,128)(2,1)}, bf16[8,224,1024]{2,1,0:T(8,128)(2,1)}, bf16[8,224,512]{2,1,0:T(8,128)(2,1)}, bf16[2,4,224,1024]{3,2,1,...) custom-call(bf16[224,8192]{1,0:T(8,128)(2,1)} %convolution_convert_f, ...), custom_call_target="tpu_custom_call" | custom-call | tf_op jit(solution)/shard_map/relay_weight/pallas_call | solution.py:328
  253.3 2.3 constant_dynamic-slice_fusion
  255.6 0.0 collective-permute-start.5
  255.6 0.6 collective-permute-start.4
  256.2 0.8 collective-permute-start.3
  257.0 13.5 %multiply_convert_fusion = bf16[2048,1024]{1,0:T(8,128)(2,1)} fusion(bf16[2048,1792]{1,0:T(8,128)(2,1)} %bitcast.54, bf16[1792,1024]{1,0:T(8,128)(2,1)} %bitcast.57, bf16[1792,1024]{1,0:T(8,128)(2,1)} %convert_element_type.55.keep), kind=kOutput, calls=%fused_computation.3 | convolution fusion | flops 7522222080 | bytes 18874368 | tf_op jit(solution)/shard_map/dot_general | solution.py:351
  270.6 0.0 copy-start.2
  270.6 1.9 constant_dynamic-slice_fusion.1
  272.5 0.7 copy-done.2
  273.2 0.0 copy-start.5
  273.2 0.0 copy-start.6
  273.2 6.2 %fusion.3 = f32[1024,1792]{1,0:T(8,128)S(1)} fusion(bf16[1024,1024]{1,0:T(8,128)(2,1)S(1)} %bitcast.62, bf16[1792,1024]{1,0:T(8,128)(2,1)} %bitcast.58, bf16[1792,1024]{1,0:T(8,128)(2,1)S(1)} %copy-done.2), kind=kOutput, calls=%fused_computation.9 | convolution fusion | flops 3759931392 | bytes 16777216 | tf_op jit(solution)/shard_map/dot_general | solution.py:356
  279.4 0.0 copy-done.5
  279.4 0.0 copy-done.6
  279.4 0.0 copy-start.8
  279.5 0.6 bitcast_multiply_fusion
  280.1 1.0 copy-done.8
  281.0 5.5 %multiply_convert_fusion.1 = bf16[1024,1792]{1,0:T(8,128)(2,1)} fusion(f32[1024,1792]{1,0:T(8,128)S(1)} %fusion.3, bf16[1024,1024]{1,0:T(8,128)(2,1)S(1)} %bitcast.66, bf16[1792,1024]{1,0:T(8,128)(2,1)S(1)} %bitcast_multiply_fusion), kind=kOutput, calls=%fused_computation.4 | convolution fusion | flops 3763601408 | bytes 16777216 | tf_op jit(solution)/shard_map/dot_general | solution.py:356
  286.5 103.3 %relay_products.1 = (bf16[8,224,256]{2,1,0:T(8,128)(2,1)}, bf16[8,160,1024]{2,1,0:T(8,128)(2,1)}, bf16[2,4,224,256]{3,2,1,0:T(8,128)(2,1)}, bf16[2,4,160,1024]{3...) custom-call(bf16[224,8192]{1,0:T(8,128)(2,1)} %convolution_convert_fusion.2.v, ...), custom_call_target="tpu_custom_call" | custom-call | tf_op jit(solution)/shard_map/relay_products/pallas_call | solution.py:364
  389.8 2.3 dynamic-slice_bitcast_fusion.2
  392.1 0.2 collective-permute-start.2
  392.4 1.0 collective-permute-start.1
  393.3 2.3 reduce.1
  395.6 3.8 reduce_sum.22
  399.4 0.0 copy-start
  399.4 0.0 copy-start.1
  399.4 0.0 collective-permute-done.5
  399.4 2.3 collective-permute-start
  401.6 0.0 collective-permute-done.4
  401.6 0.0 collective-permute-done.3
  401.6 1.4 pad_maximum_fusion
  403.0 0.1 dynamic-slice_bitcast_fusion.6
  403.1 0.1 pad_maximum_fusion.1
  403.3 0.0 copy-done
  403.3 0.0 copy-done.1
  403.3 24.5 %grad_and_step.1 = (f32[1792,1024]{1,0:T(8,128)}, f32[1792,1024]{1,0:T(8,128)}, f32[1792,1024]{1,0:T(8,128)}) custom-call(bf16[8,256,1792]{2,1,0:T(8,128)(2,1)} %get-tuple-element.21.hid, bf16[8,256,1024]{2,1,0:T(8,128)(2,1)} %get-tuple-element.23.cot, s32[1792,1024]{1,0:T(8,128)} %mask.1, bf16[1792,1024]{1,0:T(8,128)(2,1)} %bitcast.59, ...), custom_call_target="tpu_custom_call" | custom-call | flops 7516192768 | bytes 45875200 | tf_op jit(solution)/shard_map/grad_and_step/pallas_call | solution.py:386
  427.8 0.0 collective-permute-done.2
  427.8 0.0 collective-permute-done.1
  427.8 0.0 collective-permute-done
  427.8 1.5 fusion.8
  429.3 0.1 maximum_bitcast_fusion
  429.4 0.5 copy.13
  429.9 1.4 copy.14
  (1 shorter events, 0.0 us)
Async XLA Ops:
  0.7 6.2 %copy-start.3 = (f32[224,8192]{1,0:T(8,128)S(1)}, f32[224,8192]{1,0:T(8,128)}, u32[]{:S(2)}) copy-start(f32[224,8192]{1,0:T(8,128)} %param.7) | copy-start | bytes 22020100
  0.7 6.2 %copy-start.7 = (s32[224]{0:T(256)S(1)}, s32[224]{0:T(256)}, u32[]{:S(2)}) copy-start(s32[224]{0:T(256)} %param.10) | copy-start | bytes 2692
  6.9 4.4 %copy-start.4 = (f32[224,8192]{1,0:T(8,128)S(1)}, f32[224,8192]{1,0:T(8,128)}, u32[]{:S(2)}) copy-start(f32[224,8192]{1,0:T(8,128)} %param.8) | copy-start | bytes 22020100
  6.9 7.4 %slice-start = ((s8[7340032]{0:T(1024)(128)(4,1)}), s8[4194304]{0:T(1024)(128)(4,1)S(1)}, s32[]{:S(2)}) async-start(s8[7340032]{0:T(1024)(128)(4,1)} %bitcast.51), calls=%async_computation | async-start | bytes 8388608
  11.3 3.0 slice-start.1
  255.6 143.8 %collective-permute-start.5 = (bf16[2,224,256]{2,1,0:T(8,128)(2,1)}, bf16[2,224,256]{2,1,0:T(8,128)(2,1)}, u32[]{:S(2)}, u32[]{:S(2)}) collective-permute-start(bf16[2,224,256]{2,1,0:T(8,128)(2,1)} %get-tuple-element.50), channel_id=1, source_target_pairs={{0,3},{1,0},{2,1},{3,2},{4,7},{5,4},{6,5},{7,6},{8,11},{9,8},{10,9... | collective-permute-start | bytes 688136 | tf_op jit(solution)/shard_map/ppermute | solution.py:313
  255.6 146.1 %collective-permute-start.4 = (bf16[2,224,256]{2,1,0:T(8,128)(2,1)}, bf16[2,224,256]{2,1,0:T(8,128)(2,1)}, u32[]{:S(2)}, u32[]{:S(2)}) collective-permute-start(bf16[2,224,256]{2,1,0:T(8,128)(2,1)} %get-tuple-element.51), channel_id=1, source_target_pairs={{0,2},{1,3},{2,0},{3,1},{4,6},{5,7},{6,4},{7,5},{8,10},{9,11},{10,... | collective-permute-start | bytes 688136 | tf_op jit(solution)/shard_map/ppermute | solution.py:313
  256.2 145.4 %collective-permute-start.3 = (bf16[2,224,256]{2,1,0:T(8,128)(2,1)}, bf16[2,224,256]{2,1,0:T(8,128)(2,1)}, u32[]{:S(2)}, u32[]{:S(2)}) collective-permute-start(bf16[2,224,256]{2,1,0:T(8,128)(2,1)} %get-tuple-element.52), channel_id=1, source_target_pairs={{0,1},{1,2},{2,3},{3,0},{4,5},{5,6},{6,7},{7,4},{8,9},{9,10},{10,1... | collective-permute-start | bytes 688136 | tf_op jit(solution)/shard_map/ppermute | solution.py:313
  270.6 2.7 copy-start.2
  273.2 6.2 %copy-start.5 = (bf16[2,4,224,1024]{3,2,1,0:T(8,128)(2,1)S(1)}, bf16[2,4,224,1024]{3,2,1,0:T(8,128)(2,1)}, u32[]{:S(2)}) copy-start(bf16[2,4,224,1024]{3,2,1,0:T(8,128)(2,1)} %get-tuple-element.25) | copy-start | bytes 11010052
  273.2 6.2 %copy-start.6 = (bf16[1792,1024]{1,0:T(8,128)(2,1)S(1)}, bf16[1792,1024]{1,0:T(8,128)(2,1)}, u32[]{:S(2)}) copy-start(bf16[1792,1024]{1,0:T(8,128)(2,1)} %get-tuple-element.26) | copy-start | bytes 11010052
  279.4 1.6 copy-start.8
  392.1 35.7 %collective-permute-start.2 = (bf16[2,96,1024]{2,1,0:T(8,128)(2,1)}, bf16[2,96,1024]{2,1,0:T(8,128)(2,1)}, u32[]{:S(2)}, u32[]{:S(2)}) collective-permute-start(bf16[2,96,1024]{2,1,0:T(8,128)(2,1)} %get-tuple-element.43), channel_id=1, source_target_pairs={{0,3},{1,0},{2,1},{3,2},{4,7},{5,4},{6,5},{7,6},{8,11},{9,8},{10,9... | collective-permute-start | bytes 1179656 | tf_op jit(solution)/shard_map/ppermute | solution.py:313
  392.4 35.4 %collective-permute-start.1 = (bf16[2,96,1024]{2,1,0:T(8,128)(2,1)}, bf16[2,96,1024]{2,1,0:T(8,128)(2,1)}, u32[]{:S(2)}, u32[]{:S(2)}) collective-permute-start(bf16[2,96,1024]{2,1,0:T(8,128)(2,1)} %get-tuple-element.44), channel_id=1, source_target_pairs={{0,2},{1,3},{2,0},{3,1},{4,6},{5,7},{6,4},{7,5},{8,10},{9,11},{10,... | collective-permute-start | bytes 1179656 | tf_op jit(solution)/shard_map/ppermute | solution.py:313
  399.4 3.9 copy-start
  399.4 3.9 copy-start.1
  399.4 28.4 %collective-permute-start = (bf16[2,96,1024]{2,1,0:T(8,128)(2,1)}, bf16[2,96,1024]{2,1,0:T(8,128)(2,1)S(1)}, u32[]{:S(2)}, u32[]{:S(2)}) collective-permute-start(bf16[2,96,1024]{2,1,0:T(8,128)(2,1)} %get-tuple-element.42), channel_id=1, source_target_pairs={{0,1},{1,2},{2,3},{3,0},{4,5},{5,6},{6,7},{7,4},{8,9},{9,10},{10,1... | collective-permute-start | bytes 1179656 | tf_op jit(solution)/shard_map/ppermute | solution.py:313

commit v4 on v3

--- a/solution.py
+++ b/solution.py
@@ -187,9 +187,9 @@
 
     spread_w = spread(w, 0, width, w_stage, 0)
     spread_m = spread(m, 0, width, m_stage, 1)
-    spread_v = spread(v, 0, width // 2, v_stage, 2)
+    spread_v = spread(v, 0, width // 4, v_stage, 2)
     spread_c = spread(cot, 0, width, cot_out, 3)
-    spread_l = spread(v, width // 2, width // 4, v_later, 4)
+    spread_l = spread(v, width // 4, width // 2, v_later, 4)
     along_w = Along(nf, nt, w_stage, w_out, z_send.at[0], z_recv.at[0], local.at[0])
     along_m = Along(nf, nt, m_stage, m_out, z_send.at[1], z_recv.at[1], local.at[1])
     along_v = Along(nf, nt, v_stage, v_out, z_send.at[2], z_recv.at[2], local.at[2])
@@ -277,7 +277,7 @@
             total = part if total is None else total + part
         kept = mask[:, cols] != 0
         grad = jnp.where(kept, total, 0.0)
-        second = (va[:, cols] if c < 2 else vl[...] if c == 2 else vb[...]).astype(f32)
+        second = (va[...] if c == 0 else vb[...] if c == 3 else vl[:, (c - 1) * piece : c * piece]).astype(f32)
         weight = w[:, cols].astype(f32)
         first = beta_first * m[:, cols].astype(f32) + (1.0 - beta_first) * grad
         second = beta_second * second + (1.0 - beta_second) * grad * grad
@@ -323,14 +323,14 @@
     t = lax.axis_index("tensor")
     half = width // 2
     stage, landed = shape(nf, band, width), shape(g, nt, band, width)
-    stage_half, landed_half = shape(nf, band, half), shape(g, nt, band, half)
+    stage_part, landed_part = shape(nf, band, width // 4), shape(g, nt, band, width // 4)
     keep = mask.astype(bf16)
     moved = pl.pallas_call(
         functools.partial(first_kernel, nf, nt, width),
         out_shape=(
-            stage, stage, stage_half, landed, landed, landed_half, shape(nf, tokens, rows), shape(nf, tokens, width),
+            stage, stage, stage_part, landed, landed, landed_part, shape(nf, tokens, rows), shape(nf, tokens, width),
             landed, shape(nf // 2, tokens, width), shape(rows, width),
-            shape(nf, band, width // 4),
+            shape(nf, band, half),
         ),
         in_specs=[ANY] * 6,
         out_specs=(ANY,) * 12,
@@ -390,7 +390,7 @@
         in_specs=[
             pl.BlockSpec((nf, tokens, tile), lambda r: (0, 0, r)),
             pl.BlockSpec((nf, tokens, width), lambda r: (0, 0, 0)),
-            whole(width), whole(width), whole(width), whole(half), whole(width // 4), whole(width // 4),
+            whole(width), whole(width), whole(width), whole(width // 4), whole(half), whole(width // 4),
         ],
         out_specs=(whole(width),) * 3,
         compiler_params=pltpu.CompilerParams(vmem_limit_bytes=48 * 2**20),
@@ -400,7 +400,7 @@
         name="grad_and_step",
     )(
         hid_all, cot_all, mask, weight, m_out.reshape(rows, width),
-        va_out.reshape(rows, half), vl_out.reshape(rows, width // 4), vb_out.reshape(rows, width // 4),
+        va_out.reshape(rows, width // 4), vl_out.reshape(rows, half), vb_out.reshape(rows, width // 4),
     )
     output = jnp.concatenate(
         [jnp.sum(out_parts.astype(f32), axis=1), sum(piece.astype(f32) for piece in out_later)], axis=1

time: 436 us -> 473 us (1.085)
  waiting for transfers between devices: 0.02 us -> 58.2 us
  Pallas kernels: 364 us -> 341 us
    ppermute x6, waiting for transfers between devices: 0.02 us -> 58.2 us  [hop(): lax.ppermute(pick(j), 'tensor', [(n, (n + j) % nt) for n in range(nt)])]
    pallas_call x1, Pallas kernels: 236 us -> 216 us  [body(): pl.pallas_call(functools.partial(first_kernel, nf, nt, width), out_shape=...]
  transfers between devices with their start and end apart: 6 -> 6, of which waited for: 0 -> 5; matrix products, arithmetic and copies ran while one was open for 9% -> 2% of each run, Pallas kernels for 30% -> 0%
where the time goes in v4:
time: 473 us; the launch traced here: 468 us
  Pallas kernels  341 us (72%)
  waiting for transfers between devices  58.2 us (12%)
  matrix products  37.5 us (8%)
  local copies, waits for them, and re-layouts  13.6 us (3%)
  other arithmetic  11.2 us (2%)
  starting transfers between devices  5.68 us (1%)
    pallas_call x1, Pallas kernels, body(): pl.pallas_call(functools.partial(first_kernel, nf, nt, width), out_shape=...  216 us
    pallas_call x1, Pallas kernels, body(): pl.pallas_call(functools.partial(second_kernel, nf, nt, width), out_shape...  100 us
    ppermute x6, waiting for transfers between devices, hop(): lax.ppermute(pick(j), 'tensor', [(n, (n + j) % nt) for n in range(nt)])  58.2 us
    pallas_call x1, Pallas kernels, body(): pl.pallas_call(functools.partial(step_kernel, scale), grid=(rows // tile,...  24.5 us
    dot_general x1, matrix products, body(): jnp.dot(hid_all.reshape(nf * tokens, rows), masked, preferred_element_typ...  13.7 us
    dot_general x3, matrix products, arrange(): jnp.dot(place, saved.astype(bf16), preferred_element_type=f32).astype(bf16)  12.2 us
    dot_general x2, matrix products, back(): lax.dot_general(cot.reshape(nf // 2 * tokens, width), masked, (((1,), (1,...  11.6 us
  transfers between devices with their start and end apart: 6, of which 5 were waited for; matrix products, arithmetic and copies ran while one was open for 2% of the time, Pallas kernels for 0%

profile of v4, /device:TPU:15, one launch (start us, length us, event | category | flops | bytes accessed | tf_op | source)
XLA Modules:
  0.0 468.3 jit_solution(4372647568118705334)
XLA Ops:
  0.7 0.0 copy-start.3
  0.7 0.0 copy-start.11
  0.7 6.2 %convolution_convert_fusion.2.v = bf16[224,8192]{1,0:T(8,128)(2,1)} fusion(f32[224,8192]{1,0:T(8,128)} %param.9, s32[224]{0:T(256)} %param.10), kind=kOutput, calls=%fused_computation.2 | convolution fusion | flops 825803776 | bytes 11010944 | tf_op jit(solution)/shard_map/dot_general | solution.py:302
  6.9 0.0 copy-done.3
  6.9 0.0 copy-done.11
  6.9 0.0 copy-start.4
  6.9 0.0 slice-start
  6.9 3.0 convolution_convert_fusion.1.w
  9.9 1.4 copy-done.4
  11.3 0.0 slice-start.1
  11.3 3.0 convolution_convert_fusion.m
  14.3 0.0 slice-done
  14.3 0.0 slice-done.1
  14.3 2.9 convert_element_type.55.keep
  17.2 216.4 %relay_weight.1 = (bf16[8,224,1024]{2,1,0:T(8,128)(2,1)}, bf16[8,224,1024]{2,1,0:T(8,128)(2,1)}, bf16[8,224,256]{2,1,0:T(8,128)(2,1)}, bf16[2,4,224,1024]{3,2,1,...) custom-call(bf16[224,8192]{1,0:T(8,128)(2,1)} %convolution_convert_f, ...), custom_call_target="tpu_custom_call" | custom-call | tf_op jit(solution)/shard_map/relay_weight/pallas_call | solution.py:328
  233.6 13.7 %multiply_convert_fusion = bf16[2048,1024]{1,0:T(8,128)(2,1)} fusion(bf16[2048,1792]{1,0:T(8,128)(2,1)} %bitcast.54, bf16[1792,1024]{1,0:T(8,128)(2,1)} %bitcast.57, bf16[1792,1024]{1,0:T(8,128)(2,1)} %convert_element_type.55.keep), kind=kOutput, calls=%fused_computation.3 | convolution fusion | flops 7522222080 | bytes 18874368 | tf_op jit(solution)/shard_map/dot_general | solution.py:351
  247.3 0.0 copy-start.2
  247.3 1.9 constant_dynamic-slice_fusion.1
  249.2 0.7 copy-done.2
  250.0 0.0 copy-start.5
  250.0 0.0 copy-start.6
  250.0 6.2 %fusion.3 = f32[1024,1792]{1,0:T(8,128)S(1)} fusion(bf16[1024,1024]{1,0:T(8,128)(2,1)S(1)} %bitcast.62, bf16[1792,1024]{1,0:T(8,128)(2,1)} %bitcast.58, bf16[1792,1024]{1,0:T(8,128)(2,1)S(1)} %copy-done.2), kind=kOutput, calls=%fused_computation.11 | convolution fusion | flops 3759931392 | bytes 16777216 | tf_op jit(solution)/shard_map/dot_general | solution.py:356
  256.2 0.0 copy-done.5
  256.2 0.0 copy-done.6
  256.2 0.0 copy-start.12
  256.2 0.6 bitcast_multiply_fusion
  256.8 1.0 copy-done.12
  257.8 5.5 %multiply_convert_fusion.1 = bf16[1024,1792]{1,0:T(8,128)(2,1)} fusion(f32[1024,1792]{1,0:T(8,128)S(1)} %fusion.3, bf16[1024,1024]{1,0:T(8,128)(2,1)S(1)} %bitcast.66, bf16[1792,1024]{1,0:T(8,128)(2,1)S(1)} %bitcast_multiply_fusion), kind=kOutput, calls=%fused_computation.4 | convolution fusion | flops 3763601408 | bytes 16777216 | tf_op jit(solution)/shard_map/dot_general | solution.py:356
  263.2 100.4 %relay_products.1 = (bf16[8,224,256]{2,1,0:T(8,128)(2,1)}, bf16[8,160,1024]{2,1,0:T(8,128)(2,1)}, bf16[2,4,224,256]{3,2,1,0:T(8,128)(2,1)}, bf16[2,4,160,1024]{3...) custom-call(bf16[224,8192]{1,0:T(8,128)(2,1)} %convolution_convert_fusion.2.v, ...), custom_call_target="tpu_custom_call" | custom-call | tf_op jit(solution)/shard_map/relay_products/pallas_call | solution.py:364
  363.7 0.0 copy-start.7
  363.7 2.4 dynamic-slice_bitcast_fusion.9
  366.1 0.0 collective-permute-start.2
  366.1 1.7 collective-permute-start.1
  367.8 2.4 collective-permute-start
  370.1 2.7 constant_dynamic-slice_fusion
  372.9 0.0 collective-permute-start.5
  372.9 1.2 collective-permute-start.4
  374.1 2.0 collective-permute-done.2
  376.1 0.0 copy-start.9
  376.1 0.5 collective-permute-start.3
  376.5 0.3 copy-done.9
  376.8 0.0 copy-done.7
  376.8 0.6 reduce.1
  377.4 0.0 copy-start.10
  377.4 3.8 reduce_sum.22
  381.2 11.9 %collective-permute-done.1 = bf16[2,96,1024]{2,1,0:T(8,128)(2,1)} collective-permute-done((bf16[2,96,1024]{2,1,0:T(8,128)(2,1)}, bf16[2,96,1024]{2,1,0:T(8,128)(2,1)}, u32[]{:S(2)}, u32[]{:S(2)}) %collective-permute-start.1) | collective-permute-done | bytes 393248 | tf_op jit(solution)/shard_map/ppermute | solution.py:313
  393.1 28.1 %collective-permute-done = bf16[2,96,1024]{2,1,0:T(8,128)(2,1)} collective-permute-done((bf16[2,96,1024]{2,1,0:T(8,128)(2,1)}, bf16[2,96,1024]{2,1,0:T(8,128)(2,1)}, u32[]{:S(2)}, u32[]{:S(2)}) %collective-permute-start) | collective-permute-done | bytes 393248 | tf_op jit(solution)/shard_map/ppermute | solution.py:313
  421.2 0.0 copy-done.10
  421.2 1.5 fusion.8
  422.7 0.1 maximum_bitcast_fusion
  422.8 0.5 copy.13
  423.3 1.4 copy.14
  424.7 6.3 %collective-permute-done.5 = bf16[2,224,512]{2,1,0:T(8,128)(2,1)} collective-permute-done((bf16[2,224,512]{2,1,0:T(8,128)(2,1)}, bf16[2,224,512]{2,1,0:T(8,128)(2,1)}, u32[]{:S(2)}, u32[]{:S(2)}) %collective-permute-start.5) | collective-permute-done | bytes 458784 | tf_op jit(solution)/shard_map/ppermute | solution.py:313
  431.0 0.0 collective-permute-done.4
  431.0 9.8 %collective-permute-done.3 = bf16[2,224,512]{2,1,0:T(8,128)(2,1)} collective-permute-done((bf16[2,224,512]{2,1,0:T(8,128)(2,1)}, bf16[2,224,512]{2,1,0:T(8,128)(2,1)}, u32[]{:S(2)}, u32[]{:S(2)}) %collective-permute-start.3) | collective-permute-done | bytes 458784 | tf_op jit(solution)/shard_map/ppermute | solution.py:313
  440.9 0.0 copy-done.8
  440.9 1.5 pad_maximum_fusion
  442.4 0.0 copy-start
  442.4 0.0 copy-start.1
  442.4 0.1 dynamic-slice_bitcast_fusion.3
  442.6 0.2 pad_maximum_fusion.1
  442.8 0.8 copy-done
  443.6 0.3 copy-done.1
  443.9 24.5 %grad_and_step.1 = (f32[1792,1024]{1,0:T(8,128)}, f32[1792,1024]{1,0:T(8,128)}, f32[1792,1024]{1,0:T(8,128)}) custom-call(bf16[8,256,1792]{2,1,0:T(8,128)(2,1)} %get-tuple-element.21.hid, bf16[8,256,1024]{2,1,0:T(8,128)(2,1)} %get-tuple-element.23.cot, s32[1792,1024]{1,0:T(8,128)} %mask.1, bf16[1792,1024]{1,0:T(8,128)(2,1)} %bitcast.59, ...), custom_call_target="tpu_custom_call" | custom-call | flops 7516192768 | bytes 45875200 | tf_op jit(solution)/shard_map/grad_and_step/pallas_call | solution.py:386
  (2 shorter events, 0.0 us)
Async XLA Ops:
  0.7 6.2 %copy-start.3 = (f32[224,8192]{1,0:T(8,128)S(1)}, f32[224,8192]{1,0:T(8,128)}, u32[]{:S(2)}) copy-start(f32[224,8192]{1,0:T(8,128)} %param.7) | copy-start | bytes 22020100
  0.7 6.2 %copy-start.11 = (s32[224]{0:T(256)S(1)}, s32[224]{0:T(256)}, u32[]{:S(2)}) copy-start(s32[224]{0:T(256)} %param.10) | copy-start | bytes 2692
  6.9 4.4 copy-start.4
  6.9 7.4 %slice-start = ((s8[7340032]{0:T(1024)(128)(4,1)}), s8[4194304]{0:T(1024)(128)(4,1)S(1)}, s32[]{:S(2)}) async-start(s8[7340032]{0:T(1024)(128)(4,1)} %bitcast.51), calls=%async_computation | async-start | bytes 8388608
  11.3 3.0 slice-start.1
  247.3 2.7 copy-start.2
  250.0 6.2 %copy-start.5 = (bf16[2,4,224,1024]{3,2,1,0:T(8,128)(2,1)S(1)}, bf16[2,4,224,1024]{3,2,1,0:T(8,128)(2,1)}, u32[]{:S(2)}) copy-start(bf16[2,4,224,1024]{3,2,1,0:T(8,128)(2,1)} %get-tuple-element.25) | copy-start | bytes 11010052
  250.0 6.2 %copy-start.6 = (bf16[1792,1024]{1,0:T(8,128)(2,1)S(1)}, bf16[1792,1024]{1,0:T(8,128)(2,1)}, u32[]{:S(2)}) copy-start(bf16[1792,1024]{1,0:T(8,128)(2,1)} %get-tuple-element.26) | copy-start | bytes 11010052
  256.2 1.6 copy-start.12
  363.7 13.2 %copy-start.7 = (bf16[2,4,160,1024]{3,2,1,0:T(8,128)(2,1)S(1)}, bf16[2,4,160,1024]{3,2,1,0:T(8,128)(2,1)}, u32[]{:S(2)}) copy-start(bf16[2,4,160,1024]{3,2,1,0:T(8,128)(2,1)} %get-tuple-element.27) | copy-start | bytes 7864324
  366.1 10.0 %collective-permute-start.2 = (bf16[2,96,1024]{2,1,0:T(8,128)(2,1)S(1)}, bf16[2,96,1024]{2,1,0:T(8,128)(2,1)S(1)}, u32[]{:S(2)}, u32[]{:S(2)}) collective-permute-start(bf16[2,96,1024]{2,1,0:T(8,128)(2,1)S(1)} %get-tuple-element.51), channel_id=1, source_target_pairs={{0,3},{1,0},{2,1},{3,2},{4,7},{5,4},{6,5},{7,6},{8,11},{9,8},{10,9... | collective-permute-start | bytes 1179656 | tf_op jit(solution)/shard_map/ppermute | solution.py:313
  366.1 27.0 %collective-permute-start.1 = (bf16[2,96,1024]{2,1,0:T(8,128)(2,1)}, bf16[2,96,1024]{2,1,0:T(8,128)(2,1)}, u32[]{:S(2)}, u32[]{:S(2)}) collective-permute-start(bf16[2,96,1024]{2,1,0:T(8,128)(2,1)} %get-tuple-element.52), channel_id=1, source_target_pairs={{0,2},{1,3},{2,0},{3,1},{4,6},{5,7},{6,4},{7,5},{8,10},{9,11},{10,... | collective-permute-start | bytes 1179656 | tf_op jit(solution)/shard_map/ppermute | solution.py:313
  367.8 53.4 %collective-permute-start = (bf16[2,96,1024]{2,1,0:T(8,128)(2,1)}, bf16[2,96,1024]{2,1,0:T(8,128)(2,1)}, u32[]{:S(2)}, u32[]{:S(2)}) collective-permute-start(bf16[2,96,1024]{2,1,0:T(8,128)(2,1)} %get-tuple-element.50), channel_id=1, source_target_pairs={{0,1},{1,2},{2,3},{3,0},{4,5},{5,6},{6,7},{7,4},{8,9},{9,10},{10,1... | collective-permute-start | bytes 1179656 | tf_op jit(solution)/shard_map/ppermute | solution.py:313
  372.9 58.1 %collective-permute-start.5 = (bf16[2,224,512]{2,1,0:T(8,128)(2,1)}, bf16[2,224,512]{2,1,0:T(8,128)(2,1)}, u32[]{:S(2)}, u32[]{:S(2)}) collective-permute-start(bf16[2,224,512]{2,1,0:T(8,128)(2,1)} %get-tuple-element.47), channel_id=1, source_target_pairs={{0,3},{1,0},{2,1},{3,2},{4,7},{5,4},{6,5},{7,6},{8,11},{9,8},{10,9... | collective-permute-start | bytes 1376264 | tf_op jit(solution)/shard_map/ppermute | solution.py:313
  372.9 58.2 %collective-permute-start.4 = (bf16[2,224,512]{2,1,0:T(8,128)(2,1)}, bf16[2,224,512]{2,1,0:T(8,128)(2,1)}, u32[]{:S(2)}, u32[]{:S(2)}) collective-permute-start(bf16[2,224,512]{2,1,0:T(8,128)(2,1)} %get-tuple-element.48), channel_id=1, source_target_pairs={{0,2},{1,3},{2,0},{3,1},{4,6},{5,7},{6,4},{7,5},{8,10},{9,11},{10,... | collective-permute-start | bytes 1376264 | tf_op jit(solution)/shard_map/ppermute | solution.py:313
  376.1 0.8 copy-start.9
  376.1 64.8 %collective-permute-start.3 = (bf16[2,224,512]{2,1,0:T(8,128)(2,1)}, bf16[2,224,512]{2,1,0:T(8,128)(2,1)}, u32[]{:S(2)}, u32[]{:S(2)}) collective-permute-start(bf16[2,224,512]{2,1,0:T(8,128)(2,1)} %get-tuple-element.49), channel_id=1, source_target_pairs={{0,1},{1,2},{2,3},{3,0},{4,5},{5,6},{6,7},{7,4},{8,9},{9,10},{10,1... | collective-permute-start | bytes 1376264 | tf_op jit(solution)/shard_map/ppermute | solution.py:313
  377.4 43.8 %copy-start.10 = (bf16[2,96,1024]{2,1,0:T(8,128)(2,1)S(1)}, bf16[2,96,1024]{2,1,0:T(8,128)(2,1)}, u32[]{:S(2)}) copy-start(bf16[2,96,1024]{2,1,0:T(8,128)(2,1)} %copy-done.9) | copy-start | bytes 1179652
  381.2 59.7 %copy-start.8 = (bf16[1,2,224,512]{3,2,1,0:T(8,128)(2,1)S(1)}, bf16[1,2,224,512]{3,2,1,0:T(8,128)(2,1)}, u32[]{:S(2)}) copy-start(bf16[1,2,224,512]{3,2,1,0:T(8,128)(2,1)} %get-tuple-element.46) | copy-start | bytes 1376260
  442.4 1.2 copy-start
  442.4 1.4 copy-start.1
